TPU v7x, 32 devices: a whole 2x2x4 slice. The times are simulated.
32 devices in a mesh: gx: 8 (over y, x, core), gy: 4 (over z).
Axes of the slice: x: 2, y: 2, z: 4, core: 2. Of those that a mesh axis runs over, the one named last changes fastest.
Arguments:
- fields: bfloat16 [2, 64, 16, 32, 128], P(None, None, 'gx', 'gy'), may hold values from -6 to 6
- depth_kernel: bfloat16 [64, 3, 3, 3], replicated, may hold values from -1.25 to 1.25
- point_in: bfloat16 [256, 64], replicated, may hold values from -0.75 to 0.75
- point_out: bfloat16 [64, 256], replicated, may hold values from -0.375 to 0.375
- down_kernel: bfloat16 [128, 64, 2, 2, 2], replicated, may hold values from -0.25 to 0.25
- cotangent: bfloat16 [8, 4, 1, 128, 2, 4, 64], P('gx', 'gy'), may hold values from -6 to 6
Outputs:
- coarse: bfloat16 [8, 4, 1, 128, 2, 4, 64], P('gx', 'gy')
- grad_fields: bfloat16 [2, 64, 16, 32, 128], P(None, None, 'gx', 'gy')
- grad_depth_kernel: float32 [64, 3, 3, 3], replicated
- grad_point_in: float32 [256, 64], replicated
- grad_point_out: float32 [64, 256], replicated
- grad_down_kernel: float32 [128, 64, 2, 2, 2], replicated
All inputs are finite; a program needn't handle non-finite values.
Results may differ from a plain program's by a relative error of at most 0.0066.
Values may be sent and summed in bfloat16 or wider, within the bound.
No kernel may reach another device: no remote copies, remote signals or barrier semaphores. Data moves between devices by JAX's collectives and lax.ppermute only.
A program may use at most 192 MiB of HBM per device.

v0:
```python
import functools
import math

import jax
import jax.numpy as jnp
from jax import lax
from jax.experimental import pallas as pl
from jax.experimental.pallas import tpu as pltpu
from jax.sharding import PartitionSpec as P

GRIDC = 4
F32 = jnp.float32
BF16 = jnp.bfloat16
MIB = 1024 * 1024
STACK = 10
GELU_C = math.sqrt(2.0 / math.pi)
GELU_A = 0.044715


def dot(a, b, ca, cb):
    return lax.dot_general(a, b, (((ca,), (cb,)), ((), ())), preferred_element_type=F32)


def sides():
    return lax.axis_index("gx") % 2, lax.axis_index("gy") % 2


def write_pieces(row, s, Y, near, far, first, second):
    p, q = sides()
    for k, (x, plane) in enumerate(((1 - p, near), (p, far))):
        for y in range(Y):
            plane[s, y] = row(x, y)
        first[k, s] = row(x, (1 - q) * (Y - 1))
        second[k, s] = row(x, q * (Y - 1))


def piece_shapes(S, Y, C, Z):
    return [jax.ShapeDtypeStruct((S, Y, C, Z), BF16)] * 2 + [
        jax.ShapeDtypeStruct((2, S, C, Z), BF16)
    ] * 2


def params(mib):
    return pltpu.CompilerParams(vmem_limit_bytes=mib * MIB)


def in_vmem(n):
    return [pl.BlockSpec(memory_space=pltpu.VMEM)] * n


def swap_pairs(n, start):
    return [pair for i in range(start, n - 1, 2) for pair in ((i, i + 1), (i + 1, i))]


def swap_x(plane, start):
    return lax.ppermute(plane, "gx", swap_pairs(lax.axis_size("gx"), start))


def swap_y(rows, start):
    return lax.ppermute(rows, "gy", swap_pairs(lax.axis_size("gy"), start))


def halo_by_corners(pieces):
    near, far, first, second = pieces
    from_near, from_far = swap_x(near, 0), swap_x(far, 1)
    first, second = swap_y(first, 0), swap_y(second, 1)
    corner_far = swap_x(jnp.stack([first[1], second[1]]), 1)
    corner_near = swap_x(jnp.stack([first[0], second[0]]), 0)
    return [near, far, from_near, from_far, first, second, corner_near, corner_far]


def halo_by_planes(pieces):
    near, far, first, second = pieces
    from_near, from_far = swap_x(near, 0), swap_x(far, 1)
    _, q = sides()
    Y = near.shape[1]
    got = []
    for own, y, start in ((first, (1 - q) * (Y - 1), 0), (second, q * (Y - 1), 1)):
        rows = [
            lax.dynamic_index_in_dim(plane, y, 1, keepdims=False) for plane in (from_near, from_far)
        ]
        got.append(swap_y(jnp.concatenate([own, jnp.stack(rows)]), start))
    return [near, far, from_near, from_far, *got]


def fill_padded(planes, s, Fs):
    _, q = sides()
    for u, plane, (r0, k0), (r1, k1) in planes:
        Y = plane.shape[1]
        for y in range(Y):
            Fs[u * (Y + 2) + y + 1] = plane[s, y].astype(Fs.dtype)
        Fs[u * (Y + 2) + (1 - q) * (Y + 1)] = r0[k0, s].astype(Fs.dtype)
        Fs[u * (Y + 2) + q * (Y + 1)] = r1[k1, s].astype(Fs.dtype)


def fill_stack(Fs, FB, rows, Y):
    C, Z = Fs.shape[1:]
    for a in range(3):
        for b in range(3):
            at = (a * 3 + b) * C
            for r, (x, y) in enumerate(rows):
                row = Fs[(x + a) * (Y + 2) + y + b].astype(BF16)
                FB[at : at + C, r * Z : (r + 1) * Z] = row
    if FB.shape[0] > 9 * C:
        FB[9 * C :, :] = jnp.zeros((FB.shape[0] - 9 * C, FB.shape[1]), BF16)


def in_grid(x):
    p, _ = sides()
    return p if x else 1 - p


def from_left(value, lane):
    return jnp.where(lane == 0, 0.0, pltpu.roll(value, 1, 1))


def from_right(value, lane):
    Z = value.shape[1]
    return jnp.where(lane == Z - 1, 0.0, pltpu.roll(value, Z - 1, 1))


def conv_rows(taps, stack, C, Z, lane):
    acc = dot(taps, stack, 1, 0)
    rows = []
    for k in range(0, stack.shape[1], Z):
        left, mid, right = (acc[e * C : (e + 1) * C, k : k + Z] for e in range(3))
        rows.append(mid + from_left(left, lane) + from_right(right, lane))
    return rows


def conv_tile(wb, Fs, Ds, rows, Y, lane, c):
    Z = Fs.shape[2]
    weights = [wb[t, c : c + 8, :] for t in range(27)]
    for x, y in rows:
        acc = [None, None, None]
        for a in range(3):
            for b in range(3):
                f = Fs[(x + a) * (Y + 2) + y + b, c : c + 8, :]
                for e in range(3):
                    term = weights[(a * 3 + b) * 3 + e] * f
                    acc[e] = term if acc[e] is None else acc[e] + term
        total = acc[1] + from_left(acc[0], lane[:8]) + from_right(acc[2], lane[:8])
        Ds[c : c + 8, y * Z : (y + 1) * Z] = total


def split_kernel(X, Y, C, Z, f_ref, w_ref, near, far, first, second, taps_ref, wide):
    taps_ref[...] = outward_taps(w_ref)
    wide[...] = f_ref[0].astype(F32)

    def row(x, y):
        return wide[pl.ds(x * Y + y, C, stride=X * Y), :].astype(BF16)

    write_pieces(row, pl.program_id(0), Y, near, far, first, second)


def z_permutation(Z):
    fine = lax.broadcasted_iota(jnp.int32, (2 * Z, 2 * Z), 0)
    coarse = lax.broadcasted_iota(jnp.int32, (2 * Z, 2 * Z), 1)
    inner = coarse % Z
    goes = coarse // Z + (inner % (Z // 2)) * 2 + (inner // (Z // 2)) * Z
    return jnp.where(fine == goes, 1.0, 0.0).astype(BF16)


def outward_taps(w_ref):
    p, _ = sides()
    mirrored = jnp.concatenate([w_ref[:, 18:27], w_ref[:, 9:18], w_ref[:, 0:9]], axis=1)
    return jnp.where(p == 1, w_ref[...], mirrored)


def early_kernel(dims, gd_ref, w_ref, wd_ref, gm_ref, wb, Mb):
    X, Y, C, Z, H, O = dims
    NP = Y // 4
    step = pl.program_id(0)

    @pl.when(step == 0)
    def _():
        for t in range(27):
            wb[t] = jnp.broadcast_to(w_ref[:, t : t + 1], (C, Z))

    perm = z_permutation(Z)
    for X0 in range(X // 2):
        gp = dot(wd_ref[...], gd_ref[step, X0], 1, 1).astype(BF16)
        for a in range(2):
            for b in range(2):
                for p in range(NP):
                    src = ((a * 2 + b) * 2) * C
                    dst = ((a * 2 + b) * NP + p) * C
                    for e in range(2):
                        Mb[dst : dst + C, e * Z : (e + 1) * Z] = gp[
                            src + e * C : src + (e + 1) * C, p * Z : (p + 1) * Z
                        ]
        gm = dot(Mb[...], perm, 1, 1).astype(BF16)
        for a in range(2):
            for b in range(2):
                for p in range(NP):
                    src = ((a * 2 + b) * NP + p) * C
                    for q in range(2):
                        y = 2 * (2 * p + q) + b
                        gm_ref[step, in_grid(a), y] = gm[src : src + C, q * Z : (q + 1) * Z]


def plane_work(x, samples, dims, ops, put_merged):
    X, Y, C, Z, H, O = dims
    gm_ref, wb, pinT_ref, pout_ref, grad_ref, aout, ain, atap = ops[:8]
    Fs, FB, Ds, Gs, pre_s, ga_s, act_s, gp_s, pin, poutT = ops[8:]
    lane = lax.broadcasted_iota(jnp.int32, (C, Z), 1)
    for g in range(len(samples)):
        fill_stack(Fs.at[g], FB.at[g], [(x, y) for y in range(Y)], Y)
        Gs[g, 3 * C :, :] = jnp.zeros((C, Gs.shape[2]), BF16)
    chunks = [(g, range(4 * i, 4 * i + 4)) for g in range(len(samples)) for i in range(Y // 4)]

    def convolve(i):
        g, rows = chunks[i]
        cells = [(x, y) for y in rows]

        def tile(c):
            conv_tile(wb, Fs.at[g], Ds.at[g], cells, Y, lane, c)

        return [functools.partial(tile, c) for c in range(0, C, 8)]

    def grad_merged(i, part=slice(None)):
        g, rows = chunks[i]
        return jnp.concatenate([gm_ref[samples[g], x, y] for y in rows[part]], axis=1)

    def depth(i, lanes):
        g, rows = chunks[i]
        first = rows[0] * Z
        return Ds[g, :, first + lanes.start : first + lanes.stop].astype(BF16)

    halves = [(slice(0, 2), slice(0, 2 * Z)), (slice(2, 4), slice(2 * Z, 4 * Z))]

    def enter(i):
        def pre(lanes):
            pre_s[i, :, lanes] = dot(pin[...], depth(i, lanes), 1, 0)

        def ga(part, lanes):
            ga_s[i, :, lanes] = dot(poutT[...], grad_merged(i, part), 1, 0)

        steps = []
        for part, lanes in halves:
            steps += [functools.partial(pre, lanes), functools.partial(ga, part, lanes)]
        return steps

    def activate(i):
        def block(h0):
            hs = slice(h0, h0 + 16)
            pre = pre_s[i, hs, :]
            sq = pre * pre
            t = jnp.tanh(pre * (GELU_C + (GELU_C * GELU_A) * sq))
            h = 0.5 + 0.5 * t
            act = pre * h
            slope = h + act * (1.0 - h) * (2.0 * GELU_C + (6.0 * GELU_C * GELU_A) * sq)
            act_s[i, hs, :] = act.astype(BF16)
            gp_s[i, hs, :] = (ga_s[i, hs, :] * slope).astype(BF16)

        return [functools.partial(block, h0) for h0 in range(0, H, 16)]

    def leave(i):
        g, rows = chunks[i]

        def backward(part, lanes):
            grad_depth = dot(pinT_ref[...], gp_s[i, :, lanes], 1, 0).astype(BF16)
            for j, y in enumerate(rows[part]):
                row = grad_depth[:, j * Z : (j + 1) * Z]
                grad_ref[samples[g], y] = row
                value = row.astype(F32)
                shifted = from_right(value, lane), value, from_left(value, lane)
                for e, moved in enumerate(shifted):
                    Gs[g, e * C : (e + 1) * C, y * Z : (y + 1) * Z] = moved.astype(BF16)

        def forward(part, lanes):
            branch = dot(pout_ref[...], act_s[i, :, lanes], 1, 0)
            for j, y in enumerate(rows[part]):
                row = Fs[g, (x + 1) * (Y + 2) + y + 1]
                put_merged(g, y, (row + branch[:, j * Z : (j + 1) * Z]).astype(BF16))

        def out_sum():
            aout[...] += dot(grad_merged(i), act_s[i], 1, 1)

        def in_sum():
            ain[...] += dot(depth(i, slice(0, 4 * Z)), gp_s[i], 1, 1)

        def tap_sum():
            columns = slice(rows[0] * Z, (rows[-1] + 1) * Z)
            atap[...] += dot(FB[g, :, columns], Gs[g, :, columns], 1, 1)

        steps = [functools.partial(backward, *half) for half in halves]
        steps += [functools.partial(forward, *half) for half in halves]
        return steps + [out_sum, in_sum, tap_sum]

    def alternate(products, others):
        order = [((k + 0.5) / len(part), n, step) for n, part in enumerate((products, others))
                 for k, step in enumerate(part)]
        for _, _, step in sorted(order, key=lambda entry: entry[:2]):
            step()

    last = len(chunks) - 1
    alternate([], convolve(0))
    alternate(enter(0), convolve(1))
    alternate([], activate(0))
    for i in range(last + 1):
        alternate(enter(i + 1) if i < last else [], convolve(i + 2) if i + 2 <= last else [])
        alternate(leave(i), activate(i + 1) if i < last else [])


def merged_place(x, y, Y, C, Z):
    start = ((in_grid(x) * 2 + y % 2) * (Y // 4) + y // 4) * C
    q = y // 2 % 2
    return pl.ds(pl.multiple_of(start, C), C), slice(q * Z, (q + 1) * Z)


def set_up(pinT_ref, pout_ref, pin, poutT):
    pin[...] = pinT_ref[...].astype(F32).T.astype(BF16)
    poutT[...] = pout_ref[...].astype(F32).T.astype(BF16)


def near_kernel(dims, *refs):
    X, Y, C, Z, H, O = dims
    from_near, near, far, first, second, corner, gm_ref, wb, pinT_ref, pout_ref = refs[:10]
    grad_ref, Mb, aout, ain, atap = refs[10:15]
    Fs, FB, Ds, Gs, pre_s, ga_s, act_s, gp_s, pin, poutT = refs[15:]
    step = pl.program_id(0)

    @pl.when(step == 0)
    def _():
        aout[...] = jnp.zeros_like(aout)
        ain[...] = jnp.zeros_like(ain)
        atap[...] = jnp.zeros_like(atap)
        set_up(pinT_ref, pout_ref, pin, poutT)

    planes = [
        (0, from_near, (corner, 0), (corner, 1)),
        (1, near, (first, 0), (second, 0)),
        (2, far, (first, 1), (second, 1)),
    ]
    samples = [step * Fs.shape[0] + g for g in range(Fs.shape[0])]
    for g, sample in enumerate(samples):
        fill_padded(planes, sample, Fs.at[g])

    def put_merged(g, y, value):
        rows, lanes = merged_place(0, y, Y, C, Z)
        Mb[samples[g], rows, lanes] = value

    ops = gm_ref, wb, pinT_ref, pout_ref, grad_ref, aout, ain, atap
    ops += Fs, FB, Ds, Gs, pre_s, ga_s, act_s, gp_s, pin, poutT
    plane_work(0, samples, dims, ops, put_merged)


def far_kernel(dims, *refs):
    X, Y, C, Z, H, O = dims
    NP = Y // 4
    near, far, from_far, first, second, corner, gm_ref, wb, pinT_ref, pout_ref = refs[:10]
    gd_ref, wd_ref, grad_near_ref, Mb_ref, aout_ref, ain_ref, atap_ref = refs[10:17]
    red_ref, near_ref, grad_ref, first_ref, second_ref, packed_ref = refs[17:23]
    Fs, FB, Ds, Gs, pre_s, ga_s, act_s, gp_s, pin, poutT = refs[23:33]
    Mb, Pt, atap, adown, aout, ain, rows_s = refs[33:]
    step = pl.program_id(0)

    @pl.when(step == 0)
    def _():
        aout[...] = aout_ref[...]
        ain[...] = ain_ref[...]
        atap[...] = atap_ref[...]
        adown[...] = jnp.zeros_like(adown)
        set_up(pinT_ref, pout_ref, pin, poutT)

    planes = [
        (1, near, (first, 0), (second, 0)),
        (2, far, (first, 1), (second, 1)),
        (3, from_far, (corner, 0), (corner, 1)),
    ]
    samples = [step * Fs.shape[0] + g for g in range(Fs.shape[0])]
    for g, sample in enumerate(samples):
        fill_padded(planes, sample, Fs.at[g])
        Mb[g] = Mb_ref[sample]
        near_ref[sample] = grad_near_ref[sample]

    def put_merged(g, y, value):
        rows, lanes = merged_place(1, y, Y, C, Z)
        Mb[g, rows, lanes] = value

    ops = gm_ref, wb, pinT_ref, pout_ref, grad_ref, aout, ain, atap
    ops += Fs, FB, Ds, Gs, pre_s, ga_s, act_s, gp_s, pin, poutT
    plane_work(1, samples, dims, ops, put_merged)

    _, q = sides()
    for g, sample in enumerate(samples):
        for k, plane in enumerate((grad_near_ref, grad_ref)):
            first_ref[k, sample] = plane[sample, (1 - q) * (Y - 1)]
            second_ref[k, sample] = plane[sample, q * (Y - 1)]
        pt = dot(Mb[g], z_permutation(Z), 1, 0).astype(BF16)
        for a in range(2):
            for b in range(2):
                for p in range(NP):
                    src = ((a * 2 + b) * NP + p) * C
                    for e in range(2):
                        dst = ((a * 2 + b) * 2 + e) * C
                        Pt[g, dst : dst + C, p * Z : (p + 1) * Z] = pt[
                            src : src + C, e * Z : (e + 1) * Z
                        ]
        red_ref[sample, 0] = dot(Pt[g], wd_ref[...], 0, 0).astype(BF16)
        adown[...] += dot(Pt[g], gd_ref[sample, 0], 1, 0)

    @pl.when(step == pl.num_programs(0) - 1)
    def _():
        rows_s[...] = jnp.zeros_like(rows_s)
        for k in range(8):
            rows_s[pl.ds(k, C, stride=8), :] = adown[k * C : (k + 1) * C, :]
        row = lax.broadcasted_iota(jnp.int32, (C, 4 * C), 0)
        column = lax.broadcasted_iota(jnp.int32, (C, 4 * C), 1)
        lines = []
        for ab in range(9):
            block = jnp.where(column % C == row, atap[ab * C : (ab + 1) * C, :], 0.0)
            lines.append(jnp.sum(block, axis=0, keepdims=True))
        p, _ = sides()
        at = 8 * C + 2 * C * (H // Z)
        for a in range(3):
            for b in range(3):
                line = jnp.where(p == 1, lines[a * 3 + b], lines[(2 - a) * 3 + b])
                for k in range(0, 4 * C, Z):
                    rows_s[at : at + 1, :] = line[:, k : k + Z]
                    at += 1
        packed_ref[: rows_s.shape[0], :] = rows_s[...].astype(BF16)
        at = 8 * C
        for part in (aout, ain):
            for k in range(0, H, Z):
                packed_ref[at : at + C, :] = part[:, k : k + Z].astype(BF16)
                at += C
        at = rows_s.shape[0]
        if at < packed_ref.shape[0]:
            rest = packed_ref.shape[0] - at
            packed_ref[at:, :] = jnp.zeros((rest, Z), BF16)


def adjoint_kernel(X, Y, C, Z, *refs):
    planes, (first, second) = refs[:4], refs[4:6]
    gm_ref, w_ref, out_ref, Fs, FB, wide, tap_ref = refs[6:]
    step = pl.program_id(0)

    @pl.when(step == 0)
    def _():
        row = lax.broadcasted_iota(jnp.int32, (C, STACK * C), 0)
        column = lax.broadcasted_iota(jnp.int32, (C, STACK * C), 1)
        for e in range(3):
            block = jnp.zeros((C, STACK * C), F32)
            for ab in range(9):
                t = 26 - (ab * 3 + e)
                block = jnp.where(column == row + ab * C, w_ref[:, t : t + 1], block)
            tap_ref[e * C : (e + 1) * C, :] = block.astype(BF16)

    places = (1, 2, 0, 3)
    widened = [(places[k], planes[k], (first, k), (second, k)) for k in range(4)]
    fill_padded(widened, step, Fs)
    cells = [(x, y) for x in range(X) for y in range(Y)]
    fill_stack(Fs, FB, cells, Y)
    lane = lax.broadcasted_iota(jnp.int32, (C, Z), 1)
    for r0 in range(0, X * Y, 4):
        rows = conv_rows(tap_ref[...], FB[:, r0 * Z : (r0 + 4) * Z], C, Z, lane)
        for (x, y), value in zip(cells[r0 : r0 + 4], rows):
            total = value + gm_ref[step, x, y].astype(F32)
            wide[pl.ds(in_grid(x) * Y + y, C, stride=X * Y), :] = total
    out_ref[0] = wide[...].astype(BF16)


def finish_kernel(C, Z, H, scale, every_ref, down_ref, out_ref, in_ref, taps_ref):
    down_ref[...] = every_ref[: 8 * C, :].astype(F32) * scale
    at = 8 * C
    for ref in (out_ref, in_ref):
        for k in range(0, H, Z):
            ref[:, k : k + Z] = every_ref[at : at + C, :].astype(F32) * scale
            at += C
    taps = every_ref[at : at + 32, :].astype(F32) * scale
    for a in range(3):
        for b in range(3):
            for e in range(3):
                line, k = divmod(e * C, Z)
                line += (a * 3 + b) * (4 * C // Z)
                taps_ref[a, b, e : e + 1, :] = taps[line : line + 1, k : k + C]


def sum_spread_kernel(parts_ref, out_ref):
    total = parts_ref[0].astype(F32)
    for i in range(1, parts_ref.shape[0]):
        total = total + parts_ref[i].astype(F32)
    total = total.astype(BF16)
    for j in range(out_ref.shape[0]):
        out_ref[j] = total


def sum_spread(parts, receivers):
    shape = (receivers,) + parts.shape[1:]
    return pl.pallas_call(
        sum_spread_kernel,
        in_specs=in_vmem(1),
        out_specs=in_vmem(1)[0],
        out_shape=jax.ShapeDtypeStruct(shape, BF16),
        compiler_params=params(4),
        name="sum_spread",
    )(parts)


def swap_in_group(blocks, axis):
    g = blocks.shape[0]
    if g == 1:
        return blocks
    n = lax.axis_size(axis)
    member = lax.axis_index(axis) % g
    got = [lax.dynamic_index_in_dim(blocks, member, 0, keepdims=False)]
    for k in range(1, g):
        out = lax.dynamic_index_in_dim(blocks, (member + k) % g, 0, keepdims=False)
        pairs = [(i, i - i % g + (i + k) % g) for i in range(n)]
        got.append(lax.ppermute(out, axis, pairs))
    if g == 2:
        first = member == 0
        return jnp.stack([jnp.where(first, got[0], got[1]), jnp.where(first, got[1], got[0])])
    got = jnp.stack(got)
    return jnp.take(got, (member - jnp.arange(g, dtype=jnp.int32)) % g, axis=0)


def per_device(fields, depth_kernel, point_in, point_out, down_kernel, cotangent):
    S, C, X, Y, Z = fields.shape
    assert X == 2 and Y % 4 == 0
    H, O = point_in.shape[0], down_kernel.shape[0]
    hx, hy, hz = X // 2, Y // 2, Z // 2
    nx, ny = lax.axis_size("gx"), lax.axis_size("gy")
    devices = nx * ny
    gx, gy = nx // GRIDC, ny // GRIDC
    per_group = S // (gx * gy)

    *pieces, taps = pl.pallas_call(
        functools.partial(split_kernel, X, Y, C, Z),
        grid=(S,),
        in_specs=[pl.BlockSpec((1, C * X * Y, Z), lambda s: (s, 0, 0)), *in_vmem(1)],
        out_specs=in_vmem(5),
        out_shape=piece_shapes(S, Y, C, Z) + [jax.ShapeDtypeStruct((C, 27), F32)],
        scratch_shapes=[pltpu.VMEM((C * X * Y, Z), F32)],
        compiler_params=params(6),
        name="split_fields",
    )(fields.reshape(S, C * X * Y, Z), depth_kernel.reshape(C, 27).astype(F32))


    moved = cotangent[0, 0].transpose(0, 2, 3, 4, 1)
    moved = moved.reshape(per_group, gx * hx, gy, hy * hz, O).transpose(2, 0, 1, 3, 4)
    moved = swap_in_group(moved, "gy").reshape(gy * per_group, gx, hx, hy * hz, O)
    moved = swap_in_group(moved.transpose(1, 0, 2, 3, 4), "gx")
    grad_down = moved.reshape(S, hx, hy * hz, O)

    widened = halo_by_corners(pieces)

    wd = down_kernel.transpose(2, 3, 4, 1, 0).reshape(8 * C, O)

    rows = 8 * C + 2 * C * (H // Z) + 32
    chunk = -(-rows // (8 * nx)) * 8
    cells = X * Y * Z
    dims = (X, Y, C, Z, H, O)
    grad_merged, spread = pl.pallas_call(
        functools.partial(early_kernel, dims),
        grid=(S,),
        in_specs=in_vmem(3),
        out_specs=in_vmem(2),
        out_shape=[
            jax.ShapeDtypeStruct((S, X, Y, C, Z), BF16),
            jax.ShapeDtypeStruct((27, C, Z), F32),
        ],
        scratch_shapes=[pltpu.VMEM((Y * C, 2 * Z), BF16)],
        compiler_params=params(8),
        cost_estimate=pl.CostEstimate(
            flops=S * cells * (2 * C * O + 8 * C * Z),
            bytes_accessed=4 * S * cells * C + 4 * 27 * C * Z,
            transcendentals=0,
        ),
        name="early",
    )(grad_down, taps, wd)

    G = 2 if S % 2 == 0 else 1
    chunks = G * Y // 4
    scratch = [
        pltpu.VMEM((G, (X + 2) * (Y + 2), C, Z), F32),
        pltpu.VMEM((G, 9 * C, Y * Z), BF16),
        pltpu.VMEM((G, C, Y * Z), F32),
        pltpu.VMEM((G, 4 * C, Y * Z), BF16),
        pltpu.VMEM((chunks, H, 4 * Z), F32),
        pltpu.VMEM((chunks, H, 4 * Z), F32),
        pltpu.VMEM((chunks, H, 4 * Z), BF16),
        pltpu.VMEM((chunks, H, 4 * Z), BF16),
        pltpu.VMEM((H, C), BF16),
        pltpu.VMEM((H, C), BF16),
    ]
    sums = [(C, H), (C, H), (9 * C, 4 * C)]
    cost = pl.CostEstimate(
        flops=S * cells * (6 * C * H + 27 * C * 4 * C),
        bytes_accessed=8 * S * cells * C,
        transcendentals=S * cells * H // 2,
    )
    near, far, from_near, from_far, first, second, corner_near, corner_far = widened
    common = (first, second), (grad_merged, spread, point_in.T, point_out)
    grad_near, merged, *partial_sums = pl.pallas_call(
        functools.partial(near_kernel, dims),
        grid=(S // G,),
        in_specs=in_vmem(10),
        out_specs=in_vmem(5),
        out_shape=[
            jax.ShapeDtypeStruct((S, Y, C, Z), BF16),
            jax.ShapeDtypeStruct((S, Y * C, 2 * Z), BF16),
        ]
        + [jax.ShapeDtypeStruct(shape, F32) for shape in sums],
        scratch_shapes=scratch,
        compiler_params=params(17),
        cost_estimate=cost,
        name="near_side",
    )(from_near, near, far, *common[0], corner_near, *common[1])
    reduced, *grad_pieces, packed = pl.pallas_call(
        functools.partial(far_kernel, dims),
        grid=(S // G,),
        in_specs=in_vmem(17),
        out_specs=in_vmem(6),
        out_shape=[jax.ShapeDtypeStruct((S, hx, hy * hz, O), BF16)]
        + piece_shapes(S, Y, C, Z)
        + [jax.ShapeDtypeStruct((nx * chunk, Z), BF16)],
        scratch_shapes=scratch
        + [
            pltpu.VMEM((G, Y * C, 2 * Z), BF16),
            pltpu.VMEM((G, 8 * C, hy * hz), BF16),
            pltpu.VMEM((9 * C, 4 * C), F32),
            pltpu.VMEM((8 * C, O), F32),
            pltpu.VMEM((C, H), F32),
            pltpu.VMEM((C, H), F32),
            pltpu.VMEM((rows, Z), F32),
        ],
        compiler_params=params(21),
        cost_estimate=cost,
        name="far_side",
    )(
        *(near, far, from_far, first, second, corner_far, *common[1]),
        *(grad_down, wd, grad_near, merged, *partial_sums),
    )

    grad_widened = halo_by_planes(grad_pieces)

    parts = lax.all_to_all(packed.reshape(nx, chunk, Z), "gx", 0, 0)
    parts = lax.all_to_all(sum_spread(parts, ny), "gy", 0, 0)
    share = sum_spread(parts, nx)
    share, grad_widened[0] = lax.optimization_barrier((share, grad_widened[0]))
    every = lax.all_to_all(share, "gx", 0, 0).reshape(nx * chunk, Z)

    grad_fields = pl.pallas_call(
        functools.partial(adjoint_kernel, X, Y, C, Z),
        grid=(S,),
        in_specs=in_vmem(8),
        out_specs=pl.BlockSpec((1, C * X * Y, Z), lambda s: (s, 0, 0)),
        out_shape=jax.ShapeDtypeStruct((S, C * X * Y, Z), BF16),
        scratch_shapes=[
            pltpu.VMEM(((X + 2) * (Y + 2), C, Z), BF16),
            pltpu.VMEM((STACK * C, cells), BF16),
            pltpu.VMEM((C * X * Y, Z), F32),
            pltpu.VMEM((3 * C, STACK * C), BF16),
        ],
        compiler_params=params(14),
        cost_estimate=pl.CostEstimate(
            flops=S * cells * 2 * 27 * C, bytes_accessed=8 * S * cells * C, transcendentals=0
        ),
        name="adjoint",
    )(*grad_widened, grad_merged, taps).reshape(S, C, X, Y, Z)

    moved = swap_in_group(reduced.reshape(gx, S // gx, hx, hy * hz, O), "gx")
    moved = moved.transpose(1, 0, 2, 3, 4).reshape(gy, per_group, gx * hx, hy * hz, O)
    moved = swap_in_group(moved, "gy").transpose(1, 2, 0, 3, 4)
    coarse = moved.reshape(per_group, gx * hx, gy * hy, hz, O).transpose(0, 4, 1, 2, 3)[None, None]
    scale = 1.0 / math.sqrt(S * cells * devices)
    down, outw, inw, tapw = pl.pallas_call(
        functools.partial(finish_kernel, C, Z, H, scale),
        out_shape=[
            jax.ShapeDtypeStruct((8 * C, O), F32),
            jax.ShapeDtypeStruct((C, H), F32),
            jax.ShapeDtypeStruct((C, H), F32),
            jax.ShapeDtypeStruct((3, 3, 3, C), F32),
        ],
        in_specs=in_vmem(1),
        compiler_params=params(6),
        name="finish",
    )(every)
    return (
        coarse,
        grad_fields,
        tapw.transpose(3, 0, 1, 2),
        inw.T,
        outw,
        down.reshape(C, 2, 2, 2, O).transpose(4, 0, 1, 2, 3),
    )


def solution(mesh):
    placed = (
        P(None, None, "gx", "gy", None),
        P(),
        P(),
        P(),
        P(),
        P("gx", "gy", None, None, None, None, None),
    )
    return jax.shard_map(
        per_device,
        mesh=mesh,
        in_specs=placed,
        out_specs=(
            P("gx", "gy", None, None, None, None, None),
            P(None, None, "gx", "gy", None),
            P(),
            P(),
            P(),
            P(),
        ),
        check_vma=False,
    )
```

profile of v0, /device:TPU:0, one launch (start us, length us, event | category | flops | bytes accessed | tf_op | source)
XLA Modules:
  0.0 58.5 jit_solution(6628948197241818884)
XLA Ops:
  0.6 0.7 %reshape.56 = f32[64,27]{0,1:T(8,128)S(1)} reshape(bf16[64,3,3,3]{0,3,2,1:T(4,128)(2,1)} %param.7) | data formatting | bytes 10368 | tf_op jit(solution)/shard_map/convert_element_type | solution.py:539
  1.3 0.1 copy.17.w_ref
  1.4 0.0 copy-start
  1.4 1.0 %copy-done = bf16[2,64,2,8,128]{4,3,2,1,0:T(8,128)(2,1)S(1)} copy-done((bf16[2,64,2,8,128]{4,3,2,1,0:T(8,128)(2,1)S(1)}, bf16[2,64,2,8,128]{4,3,2,1,0:T(8,128)(2,1)}, u32[]{:S(2)}) %copy-start) | copy-done | bytes 524312
  2.5 0.0 copy-start.4
  2.5 0.6 split_fields.1
  3.1 0.0 copy-start.3
  3.1 3.1 %collective-permute-start.1 = (bf16[2,2,64,128]{3,2,1,0:T(8,128)(2,1)S(1)}, bf16[2,2,64,128]{3,2,1,0:T(8,128)(2,1)S(1)}, u32[]{:S(2)}, u32[]{:S(2)}) collective-permute-start(bf16[2,2,64,128]{3,2,1,0:T(8,128)(2,1)S(1)} %get-tuple-element.32), channel_id=1, source_target_pairs={{0,1},{1,0},{2,3},{3,2},{4,5},{5,4},{6,7},{7,6},{8,9},{9,8},{10,11... | collective-permute-start | bytes 196616 | tf_op jit(solution)/shard_map/ppermute | solution.py:60
  6.1 0.0 copy-done.4
  6.1 0.1 collective-permute-start.4
  6.2 0.7 %collective-permute-start.2 = (bf16[2,2,64,128]{3,2,1,0:T(8,128)(2,1)S(1)}, bf16[2,2,64,128]{3,2,1,0:T(8,128)(2,1)S(1)}, u32[]{:S(2)}, u32[]{:S(2)}) collective-permute-start(bf16[2,2,64,128]{3,2,1,0:T(8,128)(2,1)S(1)} %get-tuple-element.33), channel_id=1, source_target_pairs={{1,2},{2,1},{5,6},{6,5},{9,10},{10,9},{13,14},{14,13},{17,18},{18,... | collective-permute-start | bytes 196616 | tf_op jit(solution)/shard_map/ppermute | solution.py:60
  6.9 0.6 collective-permute-start.5
  7.4 0.7 %collective-permute-start = (bf16[2,8,64,128]{3,2,1,0:T(8,128)(2,1)S(1)}, bf16[2,8,64,128]{3,2,1,0:T(8,128)(2,1)S(1)}, u32[]{:S(2)}, u32[]{:S(2)}) collective-permute-start(bf16[2,8,64,128]{3,2,1,0:T(8,128)(2,1)S(1)} %get-tuple-element.31.refs_2_.refs_1_), channel_id=1, source_target_pairs={{4,8},{8,4},{12,16},{16,12},{20,24},{24,20},{5,9},{9,5},{13,17},{1... | collective-permute-start | bytes 786440 | tf_op jit(solution)/shard_map/ppermute | solution.py:56
  8.1 0.0 copy-done.3
  8.2 0.2 collective-permute-done.1.refs_3_
  8.4 0.0 collective-permute-done.2.refs_4_
  8.4 2.7 %collective-permute-start.6 = (bf16[2,2,64,128]{3,2,1,0:T(8,128)(2,1)S(1)}, bf16[2,2,64,128]{3,2,1,0:T(8,128)(2,1)S(1)}, u32[]{:S(2)}, u32[]{:S(2)}) collective-permute-start(bf16[2,2,64,128]{3,2,1,0:T(8,128)(2,1)S(1)} %pad_maximum_fusion.3), channel_id=1, source_target_pairs={{0,4},{4,0},{8,12},{12,8},{16,20},{20,16},{24,28},{28,24},{1,5},{5... | collective-permute-start | bytes 196616 | tf_op jit(solution)/shard_map/ppermute | solution.py:56
  11.2 0.7 %collective-permute-start.3 = (bf16[2,2,64,128]{3,2,1,0:T(8,128)(2,1)S(1)}, bf16[2,2,64,128]{3,2,1,0:T(8,128)(2,1)S(1)}, u32[]{:S(2)}, u32[]{:S(2)}) collective-permute-start(bf16[2,2,64,128]{3,2,1,0:T(8,128)(2,1)S(1)} %pad_maximum_fusion.2), channel_id=1, source_target_pairs={{4,8},{8,4},{12,16},{16,12},{20,24},{24,20},{5,9},{9,5},{13,17},{1... | collective-permute-start | bytes 196616 | tf_op jit(solution)/shard_map/ppermute | solution.py:56
  11.8 0.0 collective-permute-done.4
  11.9 0.0 copy-start.1
  11.9 0.0 copy-start.2
  11.9 1.3 %early.1 = (bf16[2,2,8,64,128]{4,3,2,1,0:T(8,128)(2,1)S(1)}, f32[27,64,128]{2,1,0:T(8,128)S(1)}) custom-call(bf16[2,1,256,128]{3,2,1,0:T(8,128)(2,1)S(1)} %maximum_bitcast_fusion.gd_ref.refs_10_, f32[64,27]{1,0:T(8,128)S(1)} %get-tuple-element.34.w_ref.refs_7_, bf16[512,128]{1,0:T(8,128)(2,1)S(1)} %bitcast.54), custom_call_target="tpu_custom_call" | custom-call | flops 335544320 | bytes 1933312 | tf_op jit(solution)/shard_map/early/pallas_call | solution.py:556
  13.2 0.0 collective-permute-done.6.refs_5_
  13.2 0.0 collective-permute-done.5.refs_0_
  13.2 0.0 copy-done.1
  13.3 0.0 copy-done.2
  13.3 4.1 %near_side.1 = (bf16[2,8,64,128]{3,2,1,0:T(8,128)(2,1)S(1)}, bf16[2,512,256]{2,1,0:T(8,128)(2,1)S(1)}, f32[64,256]{1,0:T(8,128)S(1)}, f32[64,256]{1,0:T(8,128)S(1)}, f32[576,256]{1,0:T(8,128)S(1)}) custom-call(bf16[2,8,64,128]{3,2,1,0:T(8,128)(2,1)S(1)} %collective-permute-done.5.refs_0_, bf16[2,8,64,128]{3,2,1,0:T(8,128)(2,1)S(1)} %get-tuple-element.30.refs_1_.refs_0_, ...), custom_call_target="tpu_custom_call" | custom-call | flops 2214592512 | bytes 2097152 | tf_op jit(solution)/shard_map/near_side/pallas_call | solution.py:597
  17.4 0.0 collective-permute-done.3.refs_5_
  17.4 0.0 collective-permute-done.refs_2_
  17.4 5.3 %far_side.1 = (bf16[2,1,256,128]{3,2,1,0:T(8,128)(2,1)S(1)}, bf16[2,8,64,128]{3,2,1,0:T(8,128)(2,1)S(1)}, bf16[2,8,64,128]{3,2,1,0:T(8,128)(2,1)S(1)}, bf16[2,2,...) custom-call(bf16[2,8,64,128]{3,2,1,0:T(8,128)(2,1)S(1)} %get-tuple-element.30.refs_1_.refs_, ...), custom_call_target="tpu_custom_call" | custom-call | flops 2214592512 | bytes 2097152 | tf_op jit(solution)/shard_map/far_side/pallas_call | solution.py:612
  22.7 2.9 %collective-permute-start.8 = (bf16[2,8,64,128]{3,2,1,0:T(8,128)(2,1)S(1)}, bf16[2,8,64,128]{3,2,1,0:T(8,128)(2,1)S(1)}, u32[]{:S(2)}, u32[]{:S(2)}) collective-permute-start(bf16[2,8,64,128]{3,2,1,0:T(8,128)(2,1)S(1)} %get-tuple-element.45.refs_0_), channel_id=1, source_target_pairs={{0,4},{4,0},{8,12},{12,8},{16,20},{20,16},{24,28},{28,24},{1,5},{5... | collective-permute-start | bytes 786440 | tf_op jit(solution)/shard_map/ppermute | solution.py:56
  25.5 3.4 %all-to-all-start = ((bf16[8,104,128]{2,1,0:T(8,128)(2,1)}), bf16[8,104,128]{2,1,0:T(8,128)(2,1)S(1)}, u32[]{:S(2)}, u32[]{:S(2)}) async-start(bf16[8,104,128]{2,1,0:T(8,128)(2,1)} %bitcast.21), calls=%async_computation | async-start | bytes 425984 | tf_op jit(solution)/shard_map/all_to_all | solution.py:640
  29.0 0.7 %collective-permute-start.9 = (bf16[2,8,64,128]{3,2,1,0:T(8,128)(2,1)S(1)}, bf16[2,8,64,128]{3,2,1,0:T(8,128)(2,1)S(1)}, u32[]{:S(2)}, u32[]{:S(2)}) collective-permute-start(bf16[2,8,64,128]{3,2,1,0:T(8,128)(2,1)S(1)} %get-tuple-element.46.refs_1_), channel_id=1, source_target_pairs={{4,8},{8,4},{12,16},{16,12},{20,24},{24,20},{5,9},{9,5},{13,17},{1... | collective-permute-start | bytes 786440 | tf_op jit(solution)/shard_map/ppermute | solution.py:56
  29.7 3.3 %collective-permute-start.7 = (bf16[1,1,256,128]{3,2,1,0:T(8,128)(2,1)S(1)}, bf16[1,1,256,128]{3,2,1,0:T(8,128)(2,1)S(1)}, u32[]{:S(2)}, u32[]{:S(2)}) collective-permute-start(bf16[1,1,256,128]{3,2,1,0:T(8,128)(2,1)S(1)} %constant_dynamic-slice_fusion), channel_id=1, source_target_pairs={{0,4},{4,0},{8,12},{12,8},{16,20},{20,16},{24,28},{28,24},{1,5},{5... | collective-permute-start | bytes 196616 | tf_op jit(solution)/shard_map/ppermute | solution.py:512
  33.0 2.3 %all-to-all-done.parts_ref = bf16[8,104,128]{2,1,0:T(8,128)(2,1)S(1)} async-done(((bf16[8,104,128]{2,1,0:T(8,128)(2,1)}), bf16[8,104,128]{2,1,0:T(8,128)(2,1)S(1)}, u32[]{:S(2)}, u32[]{:S(2)}) %all-to-all-start) | async-done | bytes 213024 | tf_op jit(solution)/shard_map/all_to_all | solution.py:640
  35.3 0.7 %sum_spread.2 = bf16[4,104,128]{2,1,0:T(8,128)(2,1)} custom-call(bf16[8,104,128]{2,1,0:T(8,128)(2,1)S(1)} %all-to-all-done.parts_ref), custom_call_target="tpu_custom_call" | custom-call | tf_op jit(solution)/shard_map/sum_spread/pallas_call | solution.py:492
  36.0 5.4 %all-to-all-start.1 = ((bf16[4,104,128]{2,1,0:T(8,128)(2,1)}), bf16[4,104,128]{2,1,0:T(8,128)(2,1)S(1)}, u32[]{:S(2)}, u32[]{:S(2)}) async-start(bf16[4,104,128]{2,1,0:T(8,128)(2,1)} %sum_spread.2), calls=%async_computation.1 | async-start | bytes 212992 | tf_op jit(solution)/shard_map/all_to_all | solution.py:641
  41.4 0.0 collective-permute-done.8.refs_2_
  41.4 0.0 collective-permute-done.9.refs_3_
  41.5 0.7 %collective-permute-start.11 = (bf16[4,2,64,128]{3,2,1,0:T(8,128)(2,1)S(1)}, bf16[4,2,64,128]{3,2,1,0:T(8,128)(2,1)S(1)}, u32[]{:S(2)}, u32[]{:S(2)}) collective-permute-start(bf16[4,2,64,128]{3,2,1,0:T(8,128)(2,1)S(1)} %pad_maximum_fusion.1), channel_id=1, source_target_pairs={{1,2},{2,1},{5,6},{6,5},{9,10},{10,9},{13,14},{14,13},{17,18},{18,... | collective-permute-start | bytes 393224 | tf_op jit(solution)/shard_map/ppermute | solution.py:60
  42.2 4.8 %collective-permute-start.10 = (bf16[4,2,64,128]{3,2,1,0:T(8,128)(2,1)S(1)}, bf16[4,2,64,128]{3,2,1,0:T(8,128)(2,1)S(1)}, u32[]{:S(2)}, u32[]{:S(2)}) collective-permute-start(bf16[4,2,64,128]{3,2,1,0:T(8,128)(2,1)S(1)} %pad_maximum_fusion), channel_id=1, source_target_pairs={{0,1},{1,0},{2,3},{3,2},{4,5},{5,4},{6,7},{7,6},{8,9},{9,8},{10,11... | collective-permute-start | bytes 393224 | tf_op jit(solution)/shard_map/ppermute | solution.py:60
  47.0 0.3 all-to-all-done.1.parts_ref
  47.3 0.7 %sum_spread.3 = bf16[8,104,128]{2,1,0:T(8,128)(2,1)} custom-call(bf16[4,104,128]{2,1,0:T(8,128)(2,1)S(1)} %all-to-all-done.1.parts_ref), custom_call_target="tpu_custom_call" | custom-call | tf_op jit(solution)/shard_map/sum_spread/pallas_call | solution.py:492
  48.0 3.4 %all-to-all-start.2 = ((bf16[8,104,128]{2,1,0:T(8,128)(2,1)}), bf16[8,104,128]{2,1,0:T(8,128)(2,1)S(1)}, u32[]{:S(2)}, u32[]{:S(2)}) async-start(bf16[8,104,128]{2,1,0:T(8,128)(2,1)} %sum_spread.3), calls=%async_computation.2 | async-start | bytes 425984 | tf_op jit(solution)/shard_map/all_to_all | solution.py:644
  51.4 0.0 collective-permute-done.7
  51.4 0.7 %maximum_bitcast_fusion.1 = bf16[1,1,1,128,2,4,64]{3,6,5,4,2,1,0:T(8,128)(2,1)} fusion(bf16[1,1,4,64,128]{4,3,2,1,0:T(8,128)(2,1)S(1)} %bitcast.60, bf16[1,1,4,64,128]{4,3,2,1,0:T(8,128)(2,1)S(1)} %bitcast.59), kind=kLoop, calls=%fused_computation.1 | loop fusion | flops 65536 | bytes 262144 | tf_op jit(solution)/shard_map/broadcast_in_dim | solution.py:668
  52.1 0.0 collective-permute-done.11.refs_5_
  52.1 0.0 collective-permute-done.10.refs_4_
  52.1 3.3 %adjoint.1 = bf16[2,1024,128]{2,1,0:T(8,128)(2,1)} custom-call(bf16[2,8,64,128]{3,2,1,0:T(8,128)(2,1)S(1)} %get-tuple-element.45.refs_0_, bf16[2,8,64,128]{3,2,1,0:T(8,128)(2,1)S(1)} %get-tuple-element.46.refs_1_, bf16[2,8,64,128]{3,2,1,0:T(8,128)(2,1)S(1)} %collective-permute-done.8.refs_2_, bf16[2,8,64,128]{3,2,1,0:T(8,128)(2,1)S(1)} %collective-permute-done.9.refs_3_, ...), custom_call_target="tpu_custom_call" | custom-call | flops 14155776 | bytes 2097152 | tf_op jit(solution)/shard_map/adjoint/pallas_call | solution.py:646
  55.4 2.3 %all-to-all-done.2 = bf16[8,104,128]{2,1,0:T(8,128)(2,1)S(1)} async-done(((bf16[8,104,128]{2,1,0:T(8,128)(2,1)}), bf16[8,104,128]{2,1,0:T(8,128)(2,1)S(1)}, u32[]{:S(2)}, u32[]{:S(2)}) %all-to-all-start.2) | async-done | bytes 213024 | tf_op jit(solution)/shard_map/all_to_all | solution.py:644
  57.7 0.8 %finish.1 = (f32[512,128]{1,0:T(8,128)}, f32[64,256]{1,0:T(8,128)}, f32[64,256]{1,0:T(8,128)}, f32[3,3,3,64]{3,2,1,0:T(4,128)}) custom-call(bf16[832,128]{1,0:T(8,128)(2,1)S(1)} %bitcast.52), custom_call_target="tpu_custom_call" | custom-call | tf_op jit(solution)/shard_map/finish/pallas_call | solution.py:670
  (14 shorter events, 0.2 us)
Async XLA Ops:
  1.4 1.0 %copy-start = (bf16[2,64,2,8,128]{4,3,2,1,0:T(8,128)(2,1)S(1)}, bf16[2,64,2,8,128]{4,3,2,1,0:T(8,128)(2,1)}, u32[]{:S(2)}) copy-start(bf16[2,64,2,8,128]{4,3,2,1,0:T(8,128)(2,1)} %param.6) | copy-start | bytes 1572868
  2.5 3.7 %copy-start.4 = (bf16[1,1,1,128,2,4,64]{3,6,5,4,2,1,0:T(8,128)(2,1)S(1)}, bf16[1,1,1,128,2,4,64]{3,6,5,4,2,1,0:T(8,128)(2,1)}, u32[]{:S(2)}) copy-start(bf16[1,1,1,128,2,4,64]{3,6,5,4,2,1,0:T(8,128)(2,1)} %param.11) | copy-start | bytes 393220
  3.1 5.1 %copy-start.3 = (bf16[128,64,2,2,2]{0,4,3,2,1:T(2,128)(2,1)S(1)}, bf16[128,64,2,2,2]{0,4,3,2,1:T(2,128)(2,1)}, u32[]{:S(2)}) copy-start(bf16[128,64,2,2,2]{0,4,3,2,1:T(2,128)(2,1)} %param.10) | copy-start | bytes 393220
  3.1 5.3 %collective-permute-start.1 = (bf16[2,2,64,128]{3,2,1,0:T(8,128)(2,1)S(1)}, bf16[2,2,64,128]{3,2,1,0:T(8,128)(2,1)S(1)}, u32[]{:S(2)}, u32[]{:S(2)}) collective-permute-start(bf16[2,2,64,128]{3,2,1,0:T(8,128)(2,1)S(1)} %get-tuple-element.32), channel_id=1, source_target_pairs={{0,1},{1,0},{2,3},{3,2},{4,5},{5,4},{6,7},{7,6},{8,9},{9,8},{10,11... | collective-permute-start | bytes 196616 | tf_op jit(solution)/shard_map/ppermute | solution.py:60
  6.1 5.7 %collective-permute-start.4 = (bf16[1,1,256,128]{3,2,1,0:T(8,128)(2,1)S(1)}, bf16[1,1,256,128]{3,2,1,0:T(8,128)(2,1)S(1)}, u32[]{:S(2)}, u32[]{:S(2)}) collective-permute-start(bf16[1,1,256,128]{3,2,1,0:T(8,128)(2,1)S(1)} %dynamic-slice_bitcast_fusion), channel_id=1, source_target_pairs={{0,4},{4,0},{8,12},{12,8},{16,20},{20,16},{24,28},{28,24},{1,5},{5... | collective-permute-start | bytes 196616 | tf_op jit(solution)/shard_map/ppermute | solution.py:512
  6.2 2.2 %collective-permute-start.2 = (bf16[2,2,64,128]{3,2,1,0:T(8,128)(2,1)S(1)}, bf16[2,2,64,128]{3,2,1,0:T(8,128)(2,1)S(1)}, u32[]{:S(2)}, u32[]{:S(2)}) collective-permute-start(bf16[2,2,64,128]{3,2,1,0:T(8,128)(2,1)S(1)} %get-tuple-element.33), channel_id=1, source_target_pairs={{1,2},{2,1},{5,6},{6,5},{9,10},{10,9},{13,14},{14,13},{17,18},{18,... | collective-permute-start | bytes 196616 | tf_op jit(solution)/shard_map/ppermute | solution.py:60
  6.9 6.3 %collective-permute-start.5 = (bf16[2,8,64,128]{3,2,1,0:T(8,128)(2,1)S(1)}, bf16[2,8,64,128]{3,2,1,0:T(8,128)(2,1)S(1)}, u32[]{:S(2)}, u32[]{:S(2)}) collective-permute-start(bf16[2,8,64,128]{3,2,1,0:T(8,128)(2,1)S(1)} %get-tuple-element.30.refs_1_.refs_0_), channel_id=1, source_target_pairs={{0,4},{4,0},{8,12},{12,8},{16,20},{20,16},{24,28},{28,24},{1,5},{5... | collective-permute-start | bytes 786440 | tf_op jit(solution)/shard_map/ppermute | solution.py:56
  7.4 9.9 %collective-permute-start = (bf16[2,8,64,128]{3,2,1,0:T(8,128)(2,1)S(1)}, bf16[2,8,64,128]{3,2,1,0:T(8,128)(2,1)S(1)}, u32[]{:S(2)}, u32[]{:S(2)}) collective-permute-start(bf16[2,8,64,128]{3,2,1,0:T(8,128)(2,1)S(1)} %get-tuple-element.31.refs_2_.refs_1_), channel_id=1, source_target_pairs={{4,8},{8,4},{12,16},{16,12},{20,24},{24,20},{5,9},{9,5},{13,17},{1... | collective-permute-start | bytes 786440 | tf_op jit(solution)/shard_map/ppermute | solution.py:56
  8.4 4.8 %collective-permute-start.6 = (bf16[2,2,64,128]{3,2,1,0:T(8,128)(2,1)S(1)}, bf16[2,2,64,128]{3,2,1,0:T(8,128)(2,1)S(1)}, u32[]{:S(2)}, u32[]{:S(2)}) collective-permute-start(bf16[2,2,64,128]{3,2,1,0:T(8,128)(2,1)S(1)} %pad_maximum_fusion.3), channel_id=1, source_target_pairs={{0,4},{4,0},{8,12},{12,8},{16,20},{20,16},{24,28},{28,24},{1,5},{5... | collective-permute-start | bytes 196616 | tf_op jit(solution)/shard_map/ppermute | solution.py:56
  11.2 6.2 %collective-permute-start.3 = (bf16[2,2,64,128]{3,2,1,0:T(8,128)(2,1)S(1)}, bf16[2,2,64,128]{3,2,1,0:T(8,128)(2,1)S(1)}, u32[]{:S(2)}, u32[]{:S(2)}) collective-permute-start(bf16[2,2,64,128]{3,2,1,0:T(8,128)(2,1)S(1)} %pad_maximum_fusion.2), channel_id=1, source_target_pairs={{4,8},{8,4},{12,16},{16,12},{20,24},{24,20},{5,9},{9,5},{13,17},{1... | collective-permute-start | bytes 196616 | tf_op jit(solution)/shard_map/ppermute | solution.py:56
  11.9 1.4 %copy-start.1 = (bf16[256,64]{0,1:T(8,128)(2,1)S(1)}, bf16[256,64]{0,1:T(8,128)(2,1)}, u32[]{:S(2)}) copy-start(bf16[256,64]{0,1:T(8,128)(2,1)} %param.8) | copy-start | bytes 98308
  11.9 1.4 %copy-start.2 = (bf16[64,256]{1,0:T(8,128)(2,1)S(1)}, bf16[64,256]{1,0:T(8,128)(2,1)}, u32[]{:S(2)}) copy-start(bf16[64,256]{1,0:T(8,128)(2,1)} %refs_9_.3) | copy-start | bytes 98308
  22.7 18.7 %collective-permute-start.8 = (bf16[2,8,64,128]{3,2,1,0:T(8,128)(2,1)S(1)}, bf16[2,8,64,128]{3,2,1,0:T(8,128)(2,1)S(1)}, u32[]{:S(2)}, u32[]{:S(2)}) collective-permute-start(bf16[2,8,64,128]{3,2,1,0:T(8,128)(2,1)S(1)} %get-tuple-element.45.refs_0_), channel_id=1, source_target_pairs={{0,4},{4,0},{8,12},{12,8},{16,20},{20,16},{24,28},{28,24},{1,5},{5... | collective-permute-start | bytes 786440 | tf_op jit(solution)/shard_map/ppermute | solution.py:56
  25.5 9.7 %all-to-all-start = ((bf16[8,104,128]{2,1,0:T(8,128)(2,1)}), bf16[8,104,128]{2,1,0:T(8,128)(2,1)S(1)}, u32[]{:S(2)}, u32[]{:S(2)}) async-start(bf16[8,104,128]{2,1,0:T(8,128)(2,1)} %bitcast.21), calls=%async_computation | async-start | bytes 425984 | tf_op jit(solution)/shard_map/all_to_all | solution.py:640
  29.0 12.5 %collective-permute-start.9 = (bf16[2,8,64,128]{3,2,1,0:T(8,128)(2,1)S(1)}, bf16[2,8,64,128]{3,2,1,0:T(8,128)(2,1)S(1)}, u32[]{:S(2)}, u32[]{:S(2)}) collective-permute-start(bf16[2,8,64,128]{3,2,1,0:T(8,128)(2,1)S(1)} %get-tuple-element.46.refs_1_), channel_id=1, source_target_pairs={{4,8},{8,4},{12,16},{16,12},{20,24},{24,20},{5,9},{9,5},{13,17},{1... | collective-permute-start | bytes 786440 | tf_op jit(solution)/shard_map/ppermute | solution.py:56
  29.7 21.7 %collective-permute-start.7 = (bf16[1,1,256,128]{3,2,1,0:T(8,128)(2,1)S(1)}, bf16[1,1,256,128]{3,2,1,0:T(8,128)(2,1)S(1)}, u32[]{:S(2)}, u32[]{:S(2)}) collective-permute-start(bf16[1,1,256,128]{3,2,1,0:T(8,128)(2,1)S(1)} %constant_dynamic-slice_fusion), channel_id=1, source_target_pairs={{0,4},{4,0},{8,12},{12,8},{16,20},{20,16},{24,28},{28,24},{1,5},{5... | collective-permute-start | bytes 196616 | tf_op jit(solution)/shard_map/ppermute | solution.py:512
  36.0 11.3 %all-to-all-start.1 = ((bf16[4,104,128]{2,1,0:T(8,128)(2,1)}), bf16[4,104,128]{2,1,0:T(8,128)(2,1)S(1)}, u32[]{:S(2)}, u32[]{:S(2)}) async-start(bf16[4,104,128]{2,1,0:T(8,128)(2,1)} %sum_spread.2), calls=%async_computation.1 | async-start | bytes 212992 | tf_op jit(solution)/shard_map/all_to_all | solution.py:641
  41.5 10.6 %collective-permute-start.11 = (bf16[4,2,64,128]{3,2,1,0:T(8,128)(2,1)S(1)}, bf16[4,2,64,128]{3,2,1,0:T(8,128)(2,1)S(1)}, u32[]{:S(2)}, u32[]{:S(2)}) collective-permute-start(bf16[4,2,64,128]{3,2,1,0:T(8,128)(2,1)S(1)} %pad_maximum_fusion.1), channel_id=1, source_target_pairs={{1,2},{2,1},{5,6},{6,5},{9,10},{10,9},{13,14},{14,13},{17,18},{18,... | collective-permute-start | bytes 393224 | tf_op jit(solution)/shard_map/ppermute | solution.py:60
  42.2 9.9 %collective-permute-start.10 = (bf16[4,2,64,128]{3,2,1,0:T(8,128)(2,1)S(1)}, bf16[4,2,64,128]{3,2,1,0:T(8,128)(2,1)S(1)}, u32[]{:S(2)}, u32[]{:S(2)}) collective-permute-start(bf16[4,2,64,128]{3,2,1,0:T(8,128)(2,1)S(1)} %pad_maximum_fusion), channel_id=1, source_target_pairs={{0,1},{1,0},{2,3},{3,2},{4,5},{5,4},{6,7},{7,6},{8,9},{9,8},{10,11... | collective-permute-start | bytes 393224 | tf_op jit(solution)/shard_map/ppermute | solution.py:60
  48.0 9.7 %all-to-all-start.2 = ((bf16[8,104,128]{2,1,0:T(8,128)(2,1)}), bf16[8,104,128]{2,1,0:T(8,128)(2,1)S(1)}, u32[]{:S(2)}, u32[]{:S(2)}) async-start(bf16[8,104,128]{2,1,0:T(8,128)(2,1)} %sum_spread.3), calls=%async_computation.2 | async-start | bytes 425984 | tf_op jit(solution)/shard_map/all_to_all | solution.py:644
where the time goes:
time: 59.1 us; the launch traced here: 58.5 us
  starting transfers between devices  32.9 us (56%)
  Pallas kernels  16.7 us (28%)
  waiting for transfers between devices  5.16 us (9%)
  local copies, waits for them, and re-layouts  1.94 us (3%)
  between operations  0.96 us (2%)
  other arithmetic  0.78 us (1%)
    ppermute x4, starting transfers between devices, swap_y(): return lax.ppermute(rows, 'gy', swap_pairs(lax.axis_size('gy'), start))  9.19 us
    ppermute x6, starting transfers between devices, swap_x(): return lax.ppermute(plane, 'gx', swap_pairs(lax.axis_size('gx'), start))  8.12 us
    all_to_all x1, starting transfers between devices, per_device(): parts = lax.all_to_all(sum_spread(parts, ny), 'gy', 0, 0)  5.43 us
    pallas_call x1, Pallas kernels, per_device(): pl.pallas_call(functools.partial(far_kernel, dims), grid=(S // G,), in_sp...  5.32 us
    pallas_call x1, Pallas kernels, per_device(): pl.pallas_call(functools.partial(near_kernel, dims), grid=(S // G,), in_s...  4.08 us
    all_to_all x1, starting transfers between devices, per_device(): parts = lax.all_to_all(packed.reshape(nx, chunk, Z), 'gx', 0, 0)  3.4 us
    ppermute x2, starting transfers between devices, swap_in_group(): got.append(lax.ppermute(out, axis, pairs))  3.4 us
    all_to_all x1, starting transfers between devices, per_device(): every = lax.all_to_all(share, 'gx', 0, 0).reshape(nx * chunk, Z)  3.4 us
  transfers between devices with their start and end apart: 15, of which 4 were waited for; matrix products, arithmetic and copies ran while one was open for 1% of the time, Pallas kernels for 17%

commit v1 on v0

--- a/solution.py
+++ b/solution.py
@@ -143,8 +143,7 @@
         Ds[c : c + 8, y * Z : (y + 1) * Z] = total
 
 
-def split_kernel(X, Y, C, Z, f_ref, w_ref, near, far, first, second, taps_ref, wide):
-    taps_ref[...] = outward_taps(w_ref)
+def split_kernel(X, Y, C, Z, f_ref, near, far, first, second, wide):
     wide[...] = f_ref[0].astype(F32)
 
     def row(x, y):
@@ -161,10 +160,10 @@
     return jnp.where(fine == goes, 1.0, 0.0).astype(BF16)
 
 
-def outward_taps(w_ref):
+def outward_tap(w_ref, a, b, e):
     p, _ = sides()
-    mirrored = jnp.concatenate([w_ref[:, 18:27], w_ref[:, 9:18], w_ref[:, 0:9]], axis=1)
-    return jnp.where(p == 1, w_ref[...], mirrored)
+    here, mirrored = (w_ref[x, b, e : e + 1, :].astype(F32) for x in (a, 2 - a))
+    return jnp.where(p == 1, here, mirrored)
 
 
 def early_kernel(dims, gd_ref, w_ref, wd_ref, gm_ref, wb, Mb):
@@ -174,8 +173,13 @@
 
     @pl.when(step == 0)
     def _():
+        diagonal = lax.broadcasted_iota(jnp.int32, (C, C), 0) == lax.broadcasted_iota(
+            jnp.int32, (C, C), 1
+        )
+        ones = jnp.ones((C, Z), BF16)
         for t in range(27):
-            wb[t] = jnp.broadcast_to(w_ref[:, t : t + 1], (C, Z))
+            tap = outward_tap(w_ref, t // 9, t // 3 % 3, t % 3)
+            wb[t] = dot(jnp.where(diagonal, tap, 0.0).astype(BF16), ones, 1, 0)
 
     perm = z_permutation(Z)
     for X0 in range(X // 2):
@@ -442,10 +446,9 @@
         row = lax.broadcasted_iota(jnp.int32, (C, STACK * C), 0)
         column = lax.broadcasted_iota(jnp.int32, (C, STACK * C), 1)
         for e in range(3):
-            block = jnp.zeros((C, STACK * C), F32)
-            for ab in range(9):
-                t = 26 - (ab * 3 + e)
-                block = jnp.where(column == row + ab * C, w_ref[:, t : t + 1], block)
+            taps = [outward_tap(w_ref, 2 - k // 3, 2 - k % 3, 2 - e) for k in range(9)]
+            line = jnp.concatenate(taps + [jnp.zeros((1, C), F32)], axis=1)
+            block = jnp.where(column % C == row, line, 0.0)
             tap_ref[e * C : (e + 1) * C, :] = block.astype(BF16)
 
     places = (1, 2, 0, 3)
@@ -527,16 +530,16 @@
     gx, gy = nx // GRIDC, ny // GRIDC
     per_group = S // (gx * gy)
 
-    *pieces, taps = pl.pallas_call(
+    pieces = pl.pallas_call(
         functools.partial(split_kernel, X, Y, C, Z),
         grid=(S,),
-        in_specs=[pl.BlockSpec((1, C * X * Y, Z), lambda s: (s, 0, 0)), *in_vmem(1)],
-        out_specs=in_vmem(5),
-        out_shape=piece_shapes(S, Y, C, Z) + [jax.ShapeDtypeStruct((C, 27), F32)],
+        in_specs=[pl.BlockSpec((1, C * X * Y, Z), lambda s: (s, 0, 0))],
+        out_specs=in_vmem(4),
+        out_shape=piece_shapes(S, Y, C, Z),
         scratch_shapes=[pltpu.VMEM((C * X * Y, Z), F32)],
         compiler_params=params(6),
         name="split_fields",
-    )(fields.reshape(S, C * X * Y, Z), depth_kernel.reshape(C, 27).astype(F32))
+    )(fields.reshape(S, C * X * Y, Z))
 
 
     moved = cotangent[0, 0].transpose(0, 2, 3, 4, 1)
@@ -547,6 +550,7 @@
 
     widened = halo_by_corners(pieces)
 
+    taps = depth_kernel.transpose(1, 2, 3, 0)
     wd = down_kernel.transpose(2, 3, 4, 1, 0).reshape(8 * C, O)
 
     rows = 8 * C + 2 * C * (H // Z) + 32

time: 59.1 us -> 58.9 us (level)
    convert_element_type x2 -> x0, local copies, waits for them, and re-layouts: 0.8 us -> none  [per_device(): depth_kernel.reshape(C, 27).astype(F32)]
    unnamed x10 -> x12, local copies, waits for them, and re-layouts: 1.06 us -> 1.72 us
where the time goes in v1:
time: 58.9 us; the launch traced here: 58.3 us
  starting transfers between devices  32.9 us (56%)
  Pallas kernels  16.5 us (28%)
  waiting for transfers between devices  5.29 us (9%)
  local copies, waits for them, and re-layouts  1.79 us (3%)
  between operations  0.96 us (2%)
  other arithmetic  0.78 us (1%)
    ppermute x4, starting transfers between devices, swap_y(): return lax.ppermute(rows, 'gy', swap_pairs(lax.axis_size('gy'), start))  9.19 us
    ppermute x6, starting transfers between devices, swap_x(): return lax.ppermute(plane, 'gx', swap_pairs(lax.axis_size('gx'), start))  8.13 us
    all_to_all x1, starting transfers between devices, per_device(): parts = lax.all_to_all(sum_spread(parts, ny), 'gy', 0, 0)  5.43 us
    pallas_call x1, Pallas kernels, per_device(): pl.pallas_call(functools.partial(far_kernel, dims), grid=(S // G,), in_sp...  5.33 us
    pallas_call x1, Pallas kernels, per_device(): pl.pallas_call(functools.partial(near_kernel, dims), grid=(S // G,), in_s...  4.08 us
    all_to_all x1, starting transfers between devices, per_device(): every = lax.all_to_all(share, 'gx', 0, 0).reshape(nx * chunk, Z)  3.4 us
    all_to_all x1, starting transfers between devices, per_device(): parts = lax.all_to_all(packed.reshape(nx, chunk, Z), 'gx', 0, 0)  3.4 us
    ppermute x2, starting transfers between devices, swap_in_group(): got.append(lax.ppermute(out, axis, pairs))  3.4 us
  transfers between devices with their start and end apart: 15, of which 4 were waited for; matrix products, arithmetic and copies ran while one was open for 1% of the time, Pallas kernels for 17%

profile of v1, /device:TPU:0, one launch (start us, length us, event | category | flops | bytes accessed | tf_op | source)
XLA Modules:
  0.0 58.3 jit_solution(6250382128855408751)
XLA Ops:
  0.6 0.0 copy-start
  0.6 1.0 %copy-done = bf16[2,64,2,8,128]{4,3,2,1,0:T(8,128)(2,1)S(1)} copy-done((bf16[2,64,2,8,128]{4,3,2,1,0:T(8,128)(2,1)S(1)}, bf16[2,64,2,8,128]{4,3,2,1,0:T(8,128)(2,1)}, u32[]{:S(2)}) %copy-start) | copy-done | bytes 524312
  1.7 0.0 copy-start.5
  1.7 0.6 split_fields.1
  2.2 0.0 copy-start.4
  2.2 3.1 %collective-permute-start.1 = (bf16[2,2,64,128]{3,2,1,0:T(8,128)(2,1)S(1)}, bf16[2,2,64,128]{3,2,1,0:T(8,128)(2,1)S(1)}, u32[]{:S(2)}, u32[]{:S(2)}) collective-permute-start(bf16[2,2,64,128]{3,2,1,0:T(8,128)(2,1)S(1)} %get-tuple-element.31), channel_id=1, source_target_pairs={{0,1},{1,0},{2,3},{3,2},{4,5},{5,4},{6,7},{7,6},{8,9},{9,8},{10,11... | collective-permute-start | bytes 196616 | tf_op jit(solution)/shard_map/ppermute | solution.py:60
  5.3 0.0 copy-done.5
  5.3 0.1 collective-permute-start.4
  5.4 0.7 %collective-permute-start.2 = (bf16[2,2,64,128]{3,2,1,0:T(8,128)(2,1)S(1)}, bf16[2,2,64,128]{3,2,1,0:T(8,128)(2,1)S(1)}, u32[]{:S(2)}, u32[]{:S(2)}) collective-permute-start(bf16[2,2,64,128]{3,2,1,0:T(8,128)(2,1)S(1)} %get-tuple-element.32), channel_id=1, source_target_pairs={{1,2},{2,1},{5,6},{6,5},{9,10},{10,9},{13,14},{14,13},{17,18},{18,... | collective-permute-start | bytes 196616 | tf_op jit(solution)/shard_map/ppermute | solution.py:60
  6.1 0.6 collective-permute-start.5
  6.6 0.7 %collective-permute-start = (bf16[2,8,64,128]{3,2,1,0:T(8,128)(2,1)S(1)}, bf16[2,8,64,128]{3,2,1,0:T(8,128)(2,1)S(1)}, u32[]{:S(2)}, u32[]{:S(2)}) collective-permute-start(bf16[2,8,64,128]{3,2,1,0:T(8,128)(2,1)S(1)} %get-tuple-element.30.refs_2_.refs_1_), channel_id=1, source_target_pairs={{4,8},{8,4},{12,16},{16,12},{20,24},{24,20},{5,9},{9,5},{13,17},{1... | collective-permute-start | bytes 786440 | tf_op jit(solution)/shard_map/ppermute | solution.py:56
  7.3 0.0 copy-done.4
  7.4 0.2 collective-permute-done.1.refs_3_
  7.6 0.0 collective-permute-done.2.refs_4_
  7.6 2.7 %collective-permute-start.6 = (bf16[2,2,64,128]{3,2,1,0:T(8,128)(2,1)S(1)}, bf16[2,2,64,128]{3,2,1,0:T(8,128)(2,1)S(1)}, u32[]{:S(2)}, u32[]{:S(2)}) collective-permute-start(bf16[2,2,64,128]{3,2,1,0:T(8,128)(2,1)S(1)} %pad_maximum_fusion.3), channel_id=1, source_target_pairs={{0,4},{4,0},{8,12},{12,8},{16,20},{20,16},{24,28},{28,24},{1,5},{5... | collective-permute-start | bytes 196616 | tf_op jit(solution)/shard_map/ppermute | solution.py:56
  10.3 0.7 %collective-permute-start.3 = (bf16[2,2,64,128]{3,2,1,0:T(8,128)(2,1)S(1)}, bf16[2,2,64,128]{3,2,1,0:T(8,128)(2,1)S(1)}, u32[]{:S(2)}, u32[]{:S(2)}) collective-permute-start(bf16[2,2,64,128]{3,2,1,0:T(8,128)(2,1)S(1)} %pad_maximum_fusion.2), channel_id=1, source_target_pairs={{4,8},{8,4},{12,16},{16,12},{20,24},{24,20},{5,9},{9,5},{13,17},{1... | collective-permute-start | bytes 196616 | tf_op jit(solution)/shard_map/ppermute | solution.py:56
  11.0 0.0 collective-permute-done.4
  11.0 0.0 copy-start.1
  11.1 0.7 %copy-done.1 = bf16[64,3,3,3]{0,3,2,1:T(4,128)(2,1)S(1)} copy-done((bf16[64,3,3,3]{0,3,2,1:T(4,128)(2,1)S(1)}, bf16[64,3,3,3]{0,3,2,1:T(4,128)(2,1)}, u32[]{:S(2)}) %copy-start.1) | copy-done | bytes 3480
  11.7 0.0 copy-start.2
  11.7 0.0 copy-start.3
  11.7 1.2 %early.1 = (bf16[2,2,8,64,128]{4,3,2,1,0:T(8,128)(2,1)S(1)}, f32[27,64,128]{2,1,0:T(8,128)S(1)}) custom-call(bf16[2,1,256,128]{3,2,1,0:T(8,128)(2,1)S(1)} %maximum_bitcast_fusion.gd_ref.refs_10_, bf16[3,3,3,64]{3,2,1,0:T(4,128)(2,1)S(1)} %bitcast.55, bf16[512,128]{1,0:T(8,128)(2,1)S(1)} %bitcast.53), custom_call_target="tpu_custom_call" | custom-call | flops 335544320 | bytes 1933312 | tf_op jit(solution)/shard_map/early/pallas_call | solution.py:560
  13.0 0.0 collective-permute-done.6.refs_5_
  13.0 0.0 collective-permute-done.5.refs_0_
  13.0 0.0 copy-done.2
  13.0 0.0 copy-done.3
  13.0 4.1 %near_side.1 = (bf16[2,8,64,128]{3,2,1,0:T(8,128)(2,1)S(1)}, bf16[2,512,256]{2,1,0:T(8,128)(2,1)S(1)}, f32[64,256]{1,0:T(8,128)S(1)}, f32[64,256]{1,0:T(8,128)S(1)}, f32[576,256]{1,0:T(8,128)S(1)}) custom-call(bf16[2,8,64,128]{3,2,1,0:T(8,128)(2,1)S(1)} %collective-permute-done.5.refs_0_, bf16[2,8,64,128]{3,2,1,0:T(8,128)(2,1)S(1)} %get-tuple-element.29.refs_1_.refs_0_, ...), custom_call_target="tpu_custom_call" | custom-call | flops 2214592512 | bytes 2097152 | tf_op jit(solution)/shard_map/near_side/pallas_call | solution.py:601
  17.1 0.0 collective-permute-done.3.refs_5_
  17.1 0.0 collective-permute-done.refs_2_
  17.1 5.3 %far_side.1 = (bf16[2,1,256,128]{3,2,1,0:T(8,128)(2,1)S(1)}, bf16[2,8,64,128]{3,2,1,0:T(8,128)(2,1)S(1)}, bf16[2,8,64,128]{3,2,1,0:T(8,128)(2,1)S(1)}, bf16[2,2,...) custom-call(bf16[2,8,64,128]{3,2,1,0:T(8,128)(2,1)S(1)} %get-tuple-element.29.refs_1_.refs_, ...), custom_call_target="tpu_custom_call" | custom-call | flops 2214592512 | bytes 2097152 | tf_op jit(solution)/shard_map/far_side/pallas_call | solution.py:616
  22.5 2.9 %collective-permute-start.8 = (bf16[2,8,64,128]{3,2,1,0:T(8,128)(2,1)S(1)}, bf16[2,8,64,128]{3,2,1,0:T(8,128)(2,1)S(1)}, u32[]{:S(2)}, u32[]{:S(2)}) collective-permute-start(bf16[2,8,64,128]{3,2,1,0:T(8,128)(2,1)S(1)} %get-tuple-element.43.refs_0_), channel_id=1, source_target_pairs={{0,4},{4,0},{8,12},{12,8},{16,20},{20,16},{24,28},{28,24},{1,5},{5... | collective-permute-start | bytes 786440 | tf_op jit(solution)/shard_map/ppermute | solution.py:56
  25.3 3.4 %all-to-all-start = ((bf16[8,104,128]{2,1,0:T(8,128)(2,1)}), bf16[8,104,128]{2,1,0:T(8,128)(2,1)S(1)}, u32[]{:S(2)}, u32[]{:S(2)}) async-start(bf16[8,104,128]{2,1,0:T(8,128)(2,1)} %bitcast.22), calls=%async_computation | async-start | bytes 425984 | tf_op jit(solution)/shard_map/all_to_all | solution.py:644
  28.7 0.7 %collective-permute-start.9 = (bf16[2,8,64,128]{3,2,1,0:T(8,128)(2,1)S(1)}, bf16[2,8,64,128]{3,2,1,0:T(8,128)(2,1)S(1)}, u32[]{:S(2)}, u32[]{:S(2)}) collective-permute-start(bf16[2,8,64,128]{3,2,1,0:T(8,128)(2,1)S(1)} %get-tuple-element.44.refs_1_), channel_id=1, source_target_pairs={{4,8},{8,4},{12,16},{16,12},{20,24},{24,20},{5,9},{9,5},{13,17},{1... | collective-permute-start | bytes 786440 | tf_op jit(solution)/shard_map/ppermute | solution.py:56
  29.5 3.3 %collective-permute-start.7 = (bf16[1,1,256,128]{3,2,1,0:T(8,128)(2,1)S(1)}, bf16[1,1,256,128]{3,2,1,0:T(8,128)(2,1)S(1)}, u32[]{:S(2)}, u32[]{:S(2)}) collective-permute-start(bf16[1,1,256,128]{3,2,1,0:T(8,128)(2,1)S(1)} %constant_dynamic-slice_fusion), channel_id=1, source_target_pairs={{0,4},{4,0},{8,12},{12,8},{16,20},{20,16},{24,28},{28,24},{1,5},{5... | collective-permute-start | bytes 196616 | tf_op jit(solution)/shard_map/ppermute | solution.py:515
  32.8 2.3 %all-to-all-done.parts_ref = bf16[8,104,128]{2,1,0:T(8,128)(2,1)S(1)} async-done(((bf16[8,104,128]{2,1,0:T(8,128)(2,1)}), bf16[8,104,128]{2,1,0:T(8,128)(2,1)S(1)}, u32[]{:S(2)}, u32[]{:S(2)}) %all-to-all-start) | async-done | bytes 213024 | tf_op jit(solution)/shard_map/all_to_all | solution.py:644
  35.1 0.7 %sum_spread.2 = bf16[4,104,128]{2,1,0:T(8,128)(2,1)} custom-call(bf16[8,104,128]{2,1,0:T(8,128)(2,1)S(1)} %all-to-all-done.parts_ref), custom_call_target="tpu_custom_call" | custom-call | tf_op jit(solution)/shard_map/sum_spread/pallas_call | solution.py:495
  35.7 5.4 %all-to-all-start.1 = ((bf16[4,104,128]{2,1,0:T(8,128)(2,1)}), bf16[4,104,128]{2,1,0:T(8,128)(2,1)S(1)}, u32[]{:S(2)}, u32[]{:S(2)}) async-start(bf16[4,104,128]{2,1,0:T(8,128)(2,1)} %sum_spread.2), calls=%async_computation.1 | async-start | bytes 212992 | tf_op jit(solution)/shard_map/all_to_all | solution.py:645
  41.2 0.0 collective-permute-done.8.refs_2_
  41.2 0.0 collective-permute-done.9.refs_3_
  41.2 0.7 %collective-permute-start.11 = (bf16[4,2,64,128]{3,2,1,0:T(8,128)(2,1)S(1)}, bf16[4,2,64,128]{3,2,1,0:T(8,128)(2,1)S(1)}, u32[]{:S(2)}, u32[]{:S(2)}) collective-permute-start(bf16[4,2,64,128]{3,2,1,0:T(8,128)(2,1)S(1)} %pad_maximum_fusion.1), channel_id=1, source_target_pairs={{1,2},{2,1},{5,6},{6,5},{9,10},{10,9},{13,14},{14,13},{17,18},{18,... | collective-permute-start | bytes 393224 | tf_op jit(solution)/shard_map/ppermute | solution.py:60
  41.9 4.8 %collective-permute-start.10 = (bf16[4,2,64,128]{3,2,1,0:T(8,128)(2,1)S(1)}, bf16[4,2,64,128]{3,2,1,0:T(8,128)(2,1)S(1)}, u32[]{:S(2)}, u32[]{:S(2)}) collective-permute-start(bf16[4,2,64,128]{3,2,1,0:T(8,128)(2,1)S(1)} %pad_maximum_fusion), channel_id=1, source_target_pairs={{0,1},{1,0},{2,3},{3,2},{4,5},{5,4},{6,7},{7,6},{8,9},{9,8},{10,11... | collective-permute-start | bytes 393224 | tf_op jit(solution)/shard_map/ppermute | solution.py:60
  46.7 0.3 all-to-all-done.1.parts_ref
  47.1 0.7 %sum_spread.3 = bf16[8,104,128]{2,1,0:T(8,128)(2,1)} custom-call(bf16[4,104,128]{2,1,0:T(8,128)(2,1)S(1)} %all-to-all-done.1.parts_ref), custom_call_target="tpu_custom_call" | custom-call | tf_op jit(solution)/shard_map/sum_spread/pallas_call | solution.py:495
  47.8 3.4 %all-to-all-start.2 = ((bf16[8,104,128]{2,1,0:T(8,128)(2,1)}), bf16[8,104,128]{2,1,0:T(8,128)(2,1)S(1)}, u32[]{:S(2)}, u32[]{:S(2)}) async-start(bf16[8,104,128]{2,1,0:T(8,128)(2,1)} %sum_spread.3), calls=%async_computation.2 | async-start | bytes 425984 | tf_op jit(solution)/shard_map/all_to_all | solution.py:648
  51.2 0.0 collective-permute-done.7
  51.2 0.7 %maximum_bitcast_fusion.1 = bf16[1,1,1,128,2,4,64]{3,6,5,4,2,1,0:T(8,128)(2,1)} fusion(bf16[1,1,4,64,128]{4,3,2,1,0:T(8,128)(2,1)S(1)} %bitcast.61, bf16[1,1,4,64,128]{4,3,2,1,0:T(8,128)(2,1)S(1)} %bitcast.60), kind=kLoop, calls=%fused_computation.1 | loop fusion | flops 65536 | bytes 262144 | tf_op jit(solution)/shard_map/broadcast_in_dim | solution.py:672
  51.9 0.0 collective-permute-done.11.refs_5_
  51.9 0.0 collective-permute-done.10.refs_4_
  51.9 3.2 %adjoint.1 = bf16[2,1024,128]{2,1,0:T(8,128)(2,1)} custom-call(bf16[2,8,64,128]{3,2,1,0:T(8,128)(2,1)S(1)} %get-tuple-element.43.refs_0_, bf16[2,8,64,128]{3,2,1,0:T(8,128)(2,1)S(1)} %get-tuple-element.44.refs_1_, bf16[2,8,64,128]{3,2,1,0:T(8,128)(2,1)S(1)} %collective-permute-done.8.refs_2_, bf16[2,8,64,128]{3,2,1,0:T(8,128)(2,1)S(1)} %collective-permute-done.9.refs_3_, ...), custom_call_target="tpu_custom_call" | custom-call | flops 14155776 | bytes 2097152 | tf_op jit(solution)/shard_map/adjoint/pallas_call | solution.py:650
  55.0 2.5 %all-to-all-done.2 = bf16[8,104,128]{2,1,0:T(8,128)(2,1)S(1)} async-done(((bf16[8,104,128]{2,1,0:T(8,128)(2,1)}), bf16[8,104,128]{2,1,0:T(8,128)(2,1)S(1)}, u32[]{:S(2)}, u32[]{:S(2)}) %all-to-all-start.2) | async-done | bytes 213024 | tf_op jit(solution)/shard_map/all_to_all | solution.py:648
  57.5 0.8 %finish.1 = (f32[512,128]{1,0:T(8,128)}, f32[64,256]{1,0:T(8,128)}, f32[64,256]{1,0:T(8,128)}, f32[3,3,3,64]{3,2,1,0:T(4,128)}) custom-call(bf16[832,128]{1,0:T(8,128)(2,1)S(1)} %bitcast.51), custom_call_target="tpu_custom_call" | custom-call | tf_op jit(solution)/shard_map/finish/pallas_call | solution.py:674
  (14 shorter events, 0.2 us)
Async XLA Ops:
  0.6 1.0 %copy-start = (bf16[2,64,2,8,128]{4,3,2,1,0:T(8,128)(2,1)S(1)}, bf16[2,64,2,8,128]{4,3,2,1,0:T(8,128)(2,1)}, u32[]{:S(2)}) copy-start(bf16[2,64,2,8,128]{4,3,2,1,0:T(8,128)(2,1)} %param.6) | copy-start | bytes 1572868
  1.7 3.6 %copy-start.5 = (bf16[1,1,1,128,2,4,64]{3,6,5,4,2,1,0:T(8,128)(2,1)S(1)}, bf16[1,1,1,128,2,4,64]{3,6,5,4,2,1,0:T(8,128)(2,1)}, u32[]{:S(2)}) copy-start(bf16[1,1,1,128,2,4,64]{3,6,5,4,2,1,0:T(8,128)(2,1)} %param.11) | copy-start | bytes 393220
  2.2 5.1 %copy-start.4 = (bf16[128,64,2,2,2]{0,4,3,2,1:T(2,128)(2,1)S(1)}, bf16[128,64,2,2,2]{0,4,3,2,1:T(2,128)(2,1)}, u32[]{:S(2)}) copy-start(bf16[128,64,2,2,2]{0,4,3,2,1:T(2,128)(2,1)} %param.10) | copy-start | bytes 393220
  2.2 5.3 %collective-permute-start.1 = (bf16[2,2,64,128]{3,2,1,0:T(8,128)(2,1)S(1)}, bf16[2,2,64,128]{3,2,1,0:T(8,128)(2,1)S(1)}, u32[]{:S(2)}, u32[]{:S(2)}) collective-permute-start(bf16[2,2,64,128]{3,2,1,0:T(8,128)(2,1)S(1)} %get-tuple-element.31), channel_id=1, source_target_pairs={{0,1},{1,0},{2,3},{3,2},{4,5},{5,4},{6,7},{7,6},{8,9},{9,8},{10,11... | collective-permute-start | bytes 196616 | tf_op jit(solution)/shard_map/ppermute | solution.py:60
  5.3 5.7 %collective-permute-start.4 = (bf16[1,1,256,128]{3,2,1,0:T(8,128)(2,1)S(1)}, bf16[1,1,256,128]{3,2,1,0:T(8,128)(2,1)S(1)}, u32[]{:S(2)}, u32[]{:S(2)}) collective-permute-start(bf16[1,1,256,128]{3,2,1,0:T(8,128)(2,1)S(1)} %dynamic-slice_bitcast_fusion), channel_id=1, source_target_pairs={{0,4},{4,0},{8,12},{12,8},{16,20},{20,16},{24,28},{28,24},{1,5},{5... | collective-permute-start | bytes 196616 | tf_op jit(solution)/shard_map/ppermute | solution.py:515
  5.4 2.2 %collective-permute-start.2 = (bf16[2,2,64,128]{3,2,1,0:T(8,128)(2,1)S(1)}, bf16[2,2,64,128]{3,2,1,0:T(8,128)(2,1)S(1)}, u32[]{:S(2)}, u32[]{:S(2)}) collective-permute-start(bf16[2,2,64,128]{3,2,1,0:T(8,128)(2,1)S(1)} %get-tuple-element.32), channel_id=1, source_target_pairs={{1,2},{2,1},{5,6},{6,5},{9,10},{10,9},{13,14},{14,13},{17,18},{18,... | collective-permute-start | bytes 196616 | tf_op jit(solution)/shard_map/ppermute | solution.py:60
  6.1 6.9 %collective-permute-start.5 = (bf16[2,8,64,128]{3,2,1,0:T(8,128)(2,1)S(1)}, bf16[2,8,64,128]{3,2,1,0:T(8,128)(2,1)S(1)}, u32[]{:S(2)}, u32[]{:S(2)}) collective-permute-start(bf16[2,8,64,128]{3,2,1,0:T(8,128)(2,1)S(1)} %get-tuple-element.29.refs_1_.refs_0_), channel_id=1, source_target_pairs={{0,4},{4,0},{8,12},{12,8},{16,20},{20,16},{24,28},{28,24},{1,5},{5... | collective-permute-start | bytes 786440 | tf_op jit(solution)/shard_map/ppermute | solution.py:56
  6.6 10.5 %collective-permute-start = (bf16[2,8,64,128]{3,2,1,0:T(8,128)(2,1)S(1)}, bf16[2,8,64,128]{3,2,1,0:T(8,128)(2,1)S(1)}, u32[]{:S(2)}, u32[]{:S(2)}) collective-permute-start(bf16[2,8,64,128]{3,2,1,0:T(8,128)(2,1)S(1)} %get-tuple-element.30.refs_2_.refs_1_), channel_id=1, source_target_pairs={{4,8},{8,4},{12,16},{16,12},{20,24},{24,20},{5,9},{9,5},{13,17},{1... | collective-permute-start | bytes 786440 | tf_op jit(solution)/shard_map/ppermute | solution.py:56
  7.6 5.4 %collective-permute-start.6 = (bf16[2,2,64,128]{3,2,1,0:T(8,128)(2,1)S(1)}, bf16[2,2,64,128]{3,2,1,0:T(8,128)(2,1)S(1)}, u32[]{:S(2)}, u32[]{:S(2)}) collective-permute-start(bf16[2,2,64,128]{3,2,1,0:T(8,128)(2,1)S(1)} %pad_maximum_fusion.3), channel_id=1, source_target_pairs={{0,4},{4,0},{8,12},{12,8},{16,20},{20,16},{24,28},{28,24},{1,5},{5... | collective-permute-start | bytes 196616 | tf_op jit(solution)/shard_map/ppermute | solution.py:56
  10.3 6.8 %collective-permute-start.3 = (bf16[2,2,64,128]{3,2,1,0:T(8,128)(2,1)S(1)}, bf16[2,2,64,128]{3,2,1,0:T(8,128)(2,1)S(1)}, u32[]{:S(2)}, u32[]{:S(2)}) collective-permute-start(bf16[2,2,64,128]{3,2,1,0:T(8,128)(2,1)S(1)} %pad_maximum_fusion.2), channel_id=1, source_target_pairs={{4,8},{8,4},{12,16},{16,12},{20,24},{24,20},{5,9},{9,5},{13,17},{1... | collective-permute-start | bytes 196616 | tf_op jit(solution)/shard_map/ppermute | solution.py:56
  11.0 0.7 %copy-start.1 = (bf16[64,3,3,3]{0,3,2,1:T(4,128)(2,1)S(1)}, bf16[64,3,3,3]{0,3,2,1:T(4,128)(2,1)}, u32[]{:S(2)}) copy-start(bf16[64,3,3,3]{0,3,2,1:T(4,128)(2,1)} %param.7) | copy-start | bytes 10372
  11.7 1.3 %copy-start.2 = (bf16[256,64]{0,1:T(8,128)(2,1)S(1)}, bf16[256,64]{0,1:T(8,128)(2,1)}, u32[]{:S(2)}) copy-start(bf16[256,64]{0,1:T(8,128)(2,1)} %param.8) | copy-start | bytes 98308
  11.7 1.3 %copy-start.3 = (bf16[64,256]{1,0:T(8,128)(2,1)S(1)}, bf16[64,256]{1,0:T(8,128)(2,1)}, u32[]{:S(2)}) copy-start(bf16[64,256]{1,0:T(8,128)(2,1)} %refs_9_.3) | copy-start | bytes 98308
  22.5 18.7 %collective-permute-start.8 = (bf16[2,8,64,128]{3,2,1,0:T(8,128)(2,1)S(1)}, bf16[2,8,64,128]{3,2,1,0:T(8,128)(2,1)S(1)}, u32[]{:S(2)}, u32[]{:S(2)}) collective-permute-start(bf16[2,8,64,128]{3,2,1,0:T(8,128)(2,1)S(1)} %get-tuple-element.43.refs_0_), channel_id=1, source_target_pairs={{0,4},{4,0},{8,12},{12,8},{16,20},{20,16},{24,28},{28,24},{1,5},{5... | collective-permute-start | bytes 786440 | tf_op jit(solution)/shard_map/ppermute | solution.py:56
  25.3 9.7 %all-to-all-start = ((bf16[8,104,128]{2,1,0:T(8,128)(2,1)}), bf16[8,104,128]{2,1,0:T(8,128)(2,1)S(1)}, u32[]{:S(2)}, u32[]{:S(2)}) async-start(bf16[8,104,128]{2,1,0:T(8,128)(2,1)} %bitcast.22), calls=%async_computation | async-start | bytes 425984 | tf_op jit(solution)/shard_map/all_to_all | solution.py:644
  28.7 12.5 %collective-permute-start.9 = (bf16[2,8,64,128]{3,2,1,0:T(8,128)(2,1)S(1)}, bf16[2,8,64,128]{3,2,1,0:T(8,128)(2,1)S(1)}, u32[]{:S(2)}, u32[]{:S(2)}) collective-permute-start(bf16[2,8,64,128]{3,2,1,0:T(8,128)(2,1)S(1)} %get-tuple-element.44.refs_1_), channel_id=1, source_target_pairs={{4,8},{8,4},{12,16},{16,12},{20,24},{24,20},{5,9},{9,5},{13,17},{1... | collective-permute-start | bytes 786440 | tf_op jit(solution)/shard_map/ppermute | solution.py:56
  29.5 21.7 %collective-permute-start.7 = (bf16[1,1,256,128]{3,2,1,0:T(8,128)(2,1)S(1)}, bf16[1,1,256,128]{3,2,1,0:T(8,128)(2,1)S(1)}, u32[]{:S(2)}, u32[]{:S(2)}) collective-permute-start(bf16[1,1,256,128]{3,2,1,0:T(8,128)(2,1)S(1)} %constant_dynamic-slice_fusion), channel_id=1, source_target_pairs={{0,4},{4,0},{8,12},{12,8},{16,20},{20,16},{24,28},{28,24},{1,5},{5... | collective-permute-start | bytes 196616 | tf_op jit(solution)/shard_map/ppermute | solution.py:515
  35.7 11.3 %all-to-all-start.1 = ((bf16[4,104,128]{2,1,0:T(8,128)(2,1)}), bf16[4,104,128]{2,1,0:T(8,128)(2,1)S(1)}, u32[]{:S(2)}, u32[]{:S(2)}) async-start(bf16[4,104,128]{2,1,0:T(8,128)(2,1)} %sum_spread.2), calls=%async_computation.1 | async-start | bytes 212992 | tf_op jit(solution)/shard_map/all_to_all | solution.py:645
  41.2 10.6 %collective-permute-start.11 = (bf16[4,2,64,128]{3,2,1,0:T(8,128)(2,1)S(1)}, bf16[4,2,64,128]{3,2,1,0:T(8,128)(2,1)S(1)}, u32[]{:S(2)}, u32[]{:S(2)}) collective-permute-start(bf16[4,2,64,128]{3,2,1,0:T(8,128)(2,1)S(1)} %pad_maximum_fusion.1), channel_id=1, source_target_pairs={{1,2},{2,1},{5,6},{6,5},{9,10},{10,9},{13,14},{14,13},{17,18},{18,... | collective-permute-start | bytes 393224 | tf_op jit(solution)/shard_map/ppermute | solution.py:60
  41.9 9.9 %collective-permute-start.10 = (bf16[4,2,64,128]{3,2,1,0:T(8,128)(2,1)S(1)}, bf16[4,2,64,128]{3,2,1,0:T(8,128)(2,1)S(1)}, u32[]{:S(2)}, u32[]{:S(2)}) collective-permute-start(bf16[4,2,64,128]{3,2,1,0:T(8,128)(2,1)S(1)} %pad_maximum_fusion), channel_id=1, source_target_pairs={{0,1},{1,0},{2,3},{3,2},{4,5},{5,4},{6,7},{7,6},{8,9},{9,8},{10,11... | collective-permute-start | bytes 393224 | tf_op jit(solution)/shard_map/ppermute | solution.py:60
  47.8 9.7 %all-to-all-start.2 = ((bf16[8,104,128]{2,1,0:T(8,128)(2,1)}), bf16[8,104,128]{2,1,0:T(8,128)(2,1)S(1)}, u32[]{:S(2)}, u32[]{:S(2)}) async-start(bf16[8,104,128]{2,1,0:T(8,128)(2,1)} %sum_spread.3), calls=%async_computation.2 | async-start | bytes 425984 | tf_op jit(solution)/shard_map/all_to_all | solution.py:648

commit v2 on v1

--- a/solution.py
+++ b/solution.py
@@ -143,7 +143,8 @@
         Ds[c : c + 8, y * Z : (y + 1) * Z] = total
 
 
-def split_kernel(X, Y, C, Z, f_ref, near, far, first, second, wide):
+def split_kernel(X, Y, C, Z, f_ref, w_ref, near, far, first, second, taps_ref, wide):
+    taps_ref[...] = w_ref[...]
     wide[...] = f_ref[0].astype(F32)
 
     def row(x, y):
@@ -530,16 +531,16 @@
     gx, gy = nx // GRIDC, ny // GRIDC
     per_group = S // (gx * gy)
 
-    pieces = pl.pallas_call(
+    *pieces, taps = pl.pallas_call(
         functools.partial(split_kernel, X, Y, C, Z),
         grid=(S,),
-        in_specs=[pl.BlockSpec((1, C * X * Y, Z), lambda s: (s, 0, 0))],
-        out_specs=in_vmem(4),
-        out_shape=piece_shapes(S, Y, C, Z),
+        in_specs=[pl.BlockSpec((1, C * X * Y, Z), lambda s: (s, 0, 0)), *in_vmem(1)],
+        out_specs=in_vmem(5),
+        out_shape=piece_shapes(S, Y, C, Z) + [jax.ShapeDtypeStruct((3, 3, 3, C), BF16)],
         scratch_shapes=[pltpu.VMEM((C * X * Y, Z), F32)],
         compiler_params=params(6),
         name="split_fields",
-    )(fields.reshape(S, C * X * Y, Z))
+    )(fields.reshape(S, C * X * Y, Z), depth_kernel.transpose(1, 2, 3, 0))
 
 
     moved = cotangent[0, 0].transpose(0, 2, 3, 4, 1)
@@ -550,7 +551,6 @@
 
     widened = halo_by_corners(pieces)
 
-    taps = depth_kernel.transpose(1, 2, 3, 0)
     wd = down_kernel.transpose(2, 3, 4, 1, 0).reshape(8 * C, O)
 
     rows = 8 * C + 2 * C * (H // Z) + 32

time: 58.9 us -> 58.9 us (level)
  no operation moved by 1% of the time
where the time goes in v2:
time: 58.9 us; the launch traced here: 58.3 us
  starting transfers between devices  33 us (56%)
  Pallas kernels  16.5 us (28%)
  waiting for transfers between devices  5.29 us (9%)
  local copies, waits for them, and re-layouts  1.83 us (3%)
  between operations  0.97 us (2%)
  other arithmetic  0.78 us (1%)
    ppermute x4, starting transfers between devices, swap_y(): return lax.ppermute(rows, 'gy', swap_pairs(lax.axis_size('gy'), start))  9.2 us
    ppermute x6, starting transfers between devices, swap_x(): return lax.ppermute(plane, 'gx', swap_pairs(lax.axis_size('gx'), start))  8.13 us
    all_to_all x1, starting transfers between devices, per_device(): parts = lax.all_to_all(sum_spread(parts, ny), 'gy', 0, 0)  5.43 us
    pallas_call x1, Pallas kernels, per_device(): pl.pallas_call(functools.partial(far_kernel, dims), grid=(S // G,), in_sp...  5.33 us
    pallas_call x1, Pallas kernels, per_device(): pl.pallas_call(functools.partial(near_kernel, dims), grid=(S // G,), in_s...  4.08 us
    all_to_all x1, starting transfers between devices, per_device(): parts = lax.all_to_all(packed.reshape(nx, chunk, Z), 'gx', 0, 0)  3.4 us
    ppermute x2, starting transfers between devices, swap_in_group(): got.append(lax.ppermute(out, axis, pairs))  3.4 us
    all_to_all x1, starting transfers between devices, per_device(): every = lax.all_to_all(share, 'gx', 0, 0).reshape(nx * chunk, Z)  3.4 us
  transfers between devices with their start and end apart: 15, of which 4 were waited for; matrix products, arithmetic and copies ran while one was open for 1% of the time, Pallas kernels for 17%

profile of v2, /device:TPU:0, one launch (start us, length us, event | category | flops | bytes accessed | tf_op | source)
XLA Modules:
  0.0 58.3 jit_solution(2190445614824185888)
XLA Ops:
  0.6 0.0 copy-start
  0.6 1.0 %copy-done = bf16[2,64,2,8,128]{4,3,2,1,0:T(8,128)(2,1)S(1)} copy-done((bf16[2,64,2,8,128]{4,3,2,1,0:T(8,128)(2,1)S(1)}, bf16[2,64,2,8,128]{4,3,2,1,0:T(8,128)(2,1)}, u32[]{:S(2)}) %copy-start) | copy-done | bytes 524312
  1.7 0.0 copy-start.1
  1.7 0.7 %copy-done.1 = bf16[64,3,3,3]{0,3,2,1:T(4,128)(2,1)S(1)} copy-done((bf16[64,3,3,3]{0,3,2,1:T(4,128)(2,1)S(1)}, bf16[64,3,3,3]{0,3,2,1:T(4,128)(2,1)}, u32[]{:S(2)}) %copy-start.1) | copy-done | bytes 3480
  2.4 0.0 copy-start.5
  2.4 0.5 split_fields.1
  2.9 0.0 copy-start.4
  2.9 3.1 %collective-permute-start.1 = (bf16[2,2,64,128]{3,2,1,0:T(8,128)(2,1)S(1)}, bf16[2,2,64,128]{3,2,1,0:T(8,128)(2,1)S(1)}, u32[]{:S(2)}, u32[]{:S(2)}) collective-permute-start(bf16[2,2,64,128]{3,2,1,0:T(8,128)(2,1)S(1)} %get-tuple-element.32), channel_id=1, source_target_pairs={{0,1},{1,0},{2,3},{3,2},{4,5},{5,4},{6,7},{7,6},{8,9},{9,8},{10,11... | collective-permute-start | bytes 196616 | tf_op jit(solution)/shard_map/ppermute | solution.py:60
  6.0 0.0 copy-done.5
  6.0 0.1 collective-permute-start.4
  6.1 0.7 %collective-permute-start.2 = (bf16[2,2,64,128]{3,2,1,0:T(8,128)(2,1)S(1)}, bf16[2,2,64,128]{3,2,1,0:T(8,128)(2,1)S(1)}, u32[]{:S(2)}, u32[]{:S(2)}) collective-permute-start(bf16[2,2,64,128]{3,2,1,0:T(8,128)(2,1)S(1)} %get-tuple-element.33), channel_id=1, source_target_pairs={{1,2},{2,1},{5,6},{6,5},{9,10},{10,9},{13,14},{14,13},{17,18},{18,... | collective-permute-start | bytes 196616 | tf_op jit(solution)/shard_map/ppermute | solution.py:60
  6.8 0.6 collective-permute-start.5
  7.3 0.7 %collective-permute-start = (bf16[2,8,64,128]{3,2,1,0:T(8,128)(2,1)S(1)}, bf16[2,8,64,128]{3,2,1,0:T(8,128)(2,1)S(1)}, u32[]{:S(2)}, u32[]{:S(2)}) collective-permute-start(bf16[2,8,64,128]{3,2,1,0:T(8,128)(2,1)S(1)} %get-tuple-element.31.refs_2_.refs_1_), channel_id=1, source_target_pairs={{4,8},{8,4},{12,16},{16,12},{20,24},{24,20},{5,9},{9,5},{13,17},{1... | collective-permute-start | bytes 786440 | tf_op jit(solution)/shard_map/ppermute | solution.py:56
  8.0 0.0 copy-done.4
  8.1 0.2 collective-permute-done.1.refs_3_
  8.3 0.0 collective-permute-done.2.refs_4_
  8.3 2.7 %collective-permute-start.6 = (bf16[2,2,64,128]{3,2,1,0:T(8,128)(2,1)S(1)}, bf16[2,2,64,128]{3,2,1,0:T(8,128)(2,1)S(1)}, u32[]{:S(2)}, u32[]{:S(2)}) collective-permute-start(bf16[2,2,64,128]{3,2,1,0:T(8,128)(2,1)S(1)} %pad_maximum_fusion.3), channel_id=1, source_target_pairs={{0,4},{4,0},{8,12},{12,8},{16,20},{20,16},{24,28},{28,24},{1,5},{5... | collective-permute-start | bytes 196616 | tf_op jit(solution)/shard_map/ppermute | solution.py:56
  11.0 0.7 %collective-permute-start.3 = (bf16[2,2,64,128]{3,2,1,0:T(8,128)(2,1)S(1)}, bf16[2,2,64,128]{3,2,1,0:T(8,128)(2,1)S(1)}, u32[]{:S(2)}, u32[]{:S(2)}) collective-permute-start(bf16[2,2,64,128]{3,2,1,0:T(8,128)(2,1)S(1)} %pad_maximum_fusion.2), channel_id=1, source_target_pairs={{4,8},{8,4},{12,16},{16,12},{20,24},{24,20},{5,9},{9,5},{13,17},{1... | collective-permute-start | bytes 196616 | tf_op jit(solution)/shard_map/ppermute | solution.py:56
  11.7 0.0 collective-permute-done.4
  11.8 0.0 copy-start.2
  11.8 0.0 copy-start.3
  11.8 1.3 %early.1 = (bf16[2,2,8,64,128]{4,3,2,1,0:T(8,128)(2,1)S(1)}, f32[27,64,128]{2,1,0:T(8,128)S(1)}) custom-call(bf16[2,1,256,128]{3,2,1,0:T(8,128)(2,1)S(1)} %maximum_bitcast_fusion.gd_ref.refs_10_, bf16[3,3,3,64]{3,2,1,0:T(4,128)(2,1)S(1)} %get-tuple-element.34.w_ref.refs_7_, bf16[512,128]{1,0:T(8,128)(2,1)S(1)} %bitcast.53), custom_call_target="tpu_custom_call" | custom-call | flops 335544320 | bytes 1933312 | tf_op jit(solution)/shard_map/early/pallas_call | solution.py:560
  13.1 0.0 collective-permute-done.6.refs_5_
  13.1 0.0 collective-permute-done.5.refs_0_
  13.1 0.0 copy-done.2
  13.1 0.0 copy-done.3
  13.1 4.1 %near_side.1 = (bf16[2,8,64,128]{3,2,1,0:T(8,128)(2,1)S(1)}, bf16[2,512,256]{2,1,0:T(8,128)(2,1)S(1)}, f32[64,256]{1,0:T(8,128)S(1)}, f32[64,256]{1,0:T(8,128)S(1)}, f32[576,256]{1,0:T(8,128)S(1)}) custom-call(bf16[2,8,64,128]{3,2,1,0:T(8,128)(2,1)S(1)} %collective-permute-done.5.refs_0_, bf16[2,8,64,128]{3,2,1,0:T(8,128)(2,1)S(1)} %get-tuple-element.30.refs_1_.refs_0_, ...), custom_call_target="tpu_custom_call" | custom-call | flops 2214592512 | bytes 2097152 | tf_op jit(solution)/shard_map/near_side/pallas_call | solution.py:601
  17.2 0.0 collective-permute-done.3.refs_5_
  17.2 0.0 collective-permute-done.refs_2_
  17.2 5.3 %far_side.1 = (bf16[2,1,256,128]{3,2,1,0:T(8,128)(2,1)S(1)}, bf16[2,8,64,128]{3,2,1,0:T(8,128)(2,1)S(1)}, bf16[2,8,64,128]{3,2,1,0:T(8,128)(2,1)S(1)}, bf16[2,2,...) custom-call(bf16[2,8,64,128]{3,2,1,0:T(8,128)(2,1)S(1)} %get-tuple-element.30.refs_1_.refs_, ...), custom_call_target="tpu_custom_call" | custom-call | flops 2214592512 | bytes 2097152 | tf_op jit(solution)/shard_map/far_side/pallas_call | solution.py:616
  22.5 2.9 %collective-permute-start.8 = (bf16[2,8,64,128]{3,2,1,0:T(8,128)(2,1)S(1)}, bf16[2,8,64,128]{3,2,1,0:T(8,128)(2,1)S(1)}, u32[]{:S(2)}, u32[]{:S(2)}) collective-permute-start(bf16[2,8,64,128]{3,2,1,0:T(8,128)(2,1)S(1)} %get-tuple-element.45.refs_0_), channel_id=1, source_target_pairs={{0,4},{4,0},{8,12},{12,8},{16,20},{20,16},{24,28},{28,24},{1,5},{5... | collective-permute-start | bytes 786440 | tf_op jit(solution)/shard_map/ppermute | solution.py:56
  25.4 3.4 %all-to-all-start = ((bf16[8,104,128]{2,1,0:T(8,128)(2,1)}), bf16[8,104,128]{2,1,0:T(8,128)(2,1)S(1)}, u32[]{:S(2)}, u32[]{:S(2)}) async-start(bf16[8,104,128]{2,1,0:T(8,128)(2,1)} %bitcast.22), calls=%async_computation | async-start | bytes 425984 | tf_op jit(solution)/shard_map/all_to_all | solution.py:644
  28.8 0.7 %collective-permute-start.9 = (bf16[2,8,64,128]{3,2,1,0:T(8,128)(2,1)S(1)}, bf16[2,8,64,128]{3,2,1,0:T(8,128)(2,1)S(1)}, u32[]{:S(2)}, u32[]{:S(2)}) collective-permute-start(bf16[2,8,64,128]{3,2,1,0:T(8,128)(2,1)S(1)} %get-tuple-element.46.refs_1_), channel_id=1, source_target_pairs={{4,8},{8,4},{12,16},{16,12},{20,24},{24,20},{5,9},{9,5},{13,17},{1... | collective-permute-start | bytes 786440 | tf_op jit(solution)/shard_map/ppermute | solution.py:56
  29.5 3.3 %collective-permute-start.7 = (bf16[1,1,256,128]{3,2,1,0:T(8,128)(2,1)S(1)}, bf16[1,1,256,128]{3,2,1,0:T(8,128)(2,1)S(1)}, u32[]{:S(2)}, u32[]{:S(2)}) collective-permute-start(bf16[1,1,256,128]{3,2,1,0:T(8,128)(2,1)S(1)} %constant_dynamic-slice_fusion), channel_id=1, source_target_pairs={{0,4},{4,0},{8,12},{12,8},{16,20},{20,16},{24,28},{28,24},{1,5},{5... | collective-permute-start | bytes 196616 | tf_op jit(solution)/shard_map/ppermute | solution.py:516
  32.8 2.3 %all-to-all-done.parts_ref = bf16[8,104,128]{2,1,0:T(8,128)(2,1)S(1)} async-done(((bf16[8,104,128]{2,1,0:T(8,128)(2,1)}), bf16[8,104,128]{2,1,0:T(8,128)(2,1)S(1)}, u32[]{:S(2)}, u32[]{:S(2)}) %all-to-all-start) | async-done | bytes 213024 | tf_op jit(solution)/shard_map/all_to_all | solution.py:644
  35.1 0.7 %sum_spread.2 = bf16[4,104,128]{2,1,0:T(8,128)(2,1)} custom-call(bf16[8,104,128]{2,1,0:T(8,128)(2,1)S(1)} %all-to-all-done.parts_ref), custom_call_target="tpu_custom_call" | custom-call | tf_op jit(solution)/shard_map/sum_spread/pallas_call | solution.py:496
  35.8 5.4 %all-to-all-start.1 = ((bf16[4,104,128]{2,1,0:T(8,128)(2,1)}), bf16[4,104,128]{2,1,0:T(8,128)(2,1)S(1)}, u32[]{:S(2)}, u32[]{:S(2)}) async-start(bf16[4,104,128]{2,1,0:T(8,128)(2,1)} %sum_spread.2), calls=%async_computation.1 | async-start | bytes 212992 | tf_op jit(solution)/shard_map/all_to_all | solution.py:645
  41.2 0.0 collective-permute-done.8.refs_2_
  41.2 0.0 collective-permute-done.9.refs_3_
  41.3 0.7 %collective-permute-start.11 = (bf16[4,2,64,128]{3,2,1,0:T(8,128)(2,1)S(1)}, bf16[4,2,64,128]{3,2,1,0:T(8,128)(2,1)S(1)}, u32[]{:S(2)}, u32[]{:S(2)}) collective-permute-start(bf16[4,2,64,128]{3,2,1,0:T(8,128)(2,1)S(1)} %pad_maximum_fusion.1), channel_id=1, source_target_pairs={{1,2},{2,1},{5,6},{6,5},{9,10},{10,9},{13,14},{14,13},{17,18},{18,... | collective-permute-start | bytes 393224 | tf_op jit(solution)/shard_map/ppermute | solution.py:60
  42.0 4.8 %collective-permute-start.10 = (bf16[4,2,64,128]{3,2,1,0:T(8,128)(2,1)S(1)}, bf16[4,2,64,128]{3,2,1,0:T(8,128)(2,1)S(1)}, u32[]{:S(2)}, u32[]{:S(2)}) collective-permute-start(bf16[4,2,64,128]{3,2,1,0:T(8,128)(2,1)S(1)} %pad_maximum_fusion), channel_id=1, source_target_pairs={{0,1},{1,0},{2,3},{3,2},{4,5},{5,4},{6,7},{7,6},{8,9},{9,8},{10,11... | collective-permute-start | bytes 393224 | tf_op jit(solution)/shard_map/ppermute | solution.py:60
  46.8 0.3 all-to-all-done.1.parts_ref
  47.1 0.7 %sum_spread.3 = bf16[8,104,128]{2,1,0:T(8,128)(2,1)} custom-call(bf16[4,104,128]{2,1,0:T(8,128)(2,1)S(1)} %all-to-all-done.1.parts_ref), custom_call_target="tpu_custom_call" | custom-call | tf_op jit(solution)/shard_map/sum_spread/pallas_call | solution.py:496
  47.8 3.4 %all-to-all-start.2 = ((bf16[8,104,128]{2,1,0:T(8,128)(2,1)}), bf16[8,104,128]{2,1,0:T(8,128)(2,1)S(1)}, u32[]{:S(2)}, u32[]{:S(2)}) async-start(bf16[8,104,128]{2,1,0:T(8,128)(2,1)} %sum_spread.3), calls=%async_computation.2 | async-start | bytes 425984 | tf_op jit(solution)/shard_map/all_to_all | solution.py:648
  51.2 0.0 collective-permute-done.7
  51.3 0.7 %maximum_bitcast_fusion.1 = bf16[1,1,1,128,2,4,64]{3,6,5,4,2,1,0:T(8,128)(2,1)} fusion(bf16[1,1,4,64,128]{4,3,2,1,0:T(8,128)(2,1)S(1)} %bitcast.60, bf16[1,1,4,64,128]{4,3,2,1,0:T(8,128)(2,1)S(1)} %bitcast.59), kind=kLoop, calls=%fused_computation.1 | loop fusion | flops 65536 | bytes 262144 | tf_op jit(solution)/shard_map/broadcast_in_dim | solution.py:672
  51.9 0.0 collective-permute-done.11.refs_5_
  51.9 0.0 collective-permute-done.10.refs_4_
  51.9 3.2 %adjoint.1 = bf16[2,1024,128]{2,1,0:T(8,128)(2,1)} custom-call(bf16[2,8,64,128]{3,2,1,0:T(8,128)(2,1)S(1)} %get-tuple-element.45.refs_0_, bf16[2,8,64,128]{3,2,1,0:T(8,128)(2,1)S(1)} %get-tuple-element.46.refs_1_, bf16[2,8,64,128]{3,2,1,0:T(8,128)(2,1)S(1)} %collective-permute-done.8.refs_2_, bf16[2,8,64,128]{3,2,1,0:T(8,128)(2,1)S(1)} %collective-permute-done.9.refs_3_, ...), custom_call_target="tpu_custom_call" | custom-call | flops 14155776 | bytes 2097152 | tf_op jit(solution)/shard_map/adjoint/pallas_call | solution.py:650
  55.1 2.5 %all-to-all-done.2 = bf16[8,104,128]{2,1,0:T(8,128)(2,1)S(1)} async-done(((bf16[8,104,128]{2,1,0:T(8,128)(2,1)}), bf16[8,104,128]{2,1,0:T(8,128)(2,1)S(1)}, u32[]{:S(2)}, u32[]{:S(2)}) %all-to-all-start.2) | async-done | bytes 213024 | tf_op jit(solution)/shard_map/all_to_all | solution.py:648
  57.6 0.8 %finish.1 = (f32[512,128]{1,0:T(8,128)}, f32[64,256]{1,0:T(8,128)}, f32[64,256]{1,0:T(8,128)}, f32[3,3,3,64]{3,2,1,0:T(4,128)}) custom-call(bf16[832,128]{1,0:T(8,128)(2,1)S(1)} %bitcast.51), custom_call_target="tpu_custom_call" | custom-call | tf_op jit(solution)/shard_map/finish/pallas_call | solution.py:674
  (14 shorter events, 0.2 us)
Async XLA Ops:
  0.6 1.0 %copy-start = (bf16[2,64,2,8,128]{4,3,2,1,0:T(8,128)(2,1)S(1)}, bf16[2,64,2,8,128]{4,3,2,1,0:T(8,128)(2,1)}, u32[]{:S(2)}) copy-start(bf16[2,64,2,8,128]{4,3,2,1,0:T(8,128)(2,1)} %param.6) | copy-start | bytes 1572868
  1.7 0.7 %copy-start.1 = (bf16[64,3,3,3]{0,3,2,1:T(4,128)(2,1)S(1)}, bf16[64,3,3,3]{0,3,2,1:T(4,128)(2,1)}, u32[]{:S(2)}) copy-start(bf16[64,3,3,3]{0,3,2,1:T(4,128)(2,1)} %param.7) | copy-start | bytes 10372
  2.4 3.6 %copy-start.5 = (bf16[1,1,1,128,2,4,64]{3,6,5,4,2,1,0:T(8,128)(2,1)S(1)}, bf16[1,1,1,128,2,4,64]{3,6,5,4,2,1,0:T(8,128)(2,1)}, u32[]{:S(2)}) copy-start(bf16[1,1,1,128,2,4,64]{3,6,5,4,2,1,0:T(8,128)(2,1)} %param.11) | copy-start | bytes 393220
  2.9 5.1 %copy-start.4 = (bf16[128,64,2,2,2]{0,4,3,2,1:T(2,128)(2,1)S(1)}, bf16[128,64,2,2,2]{0,4,3,2,1:T(2,128)(2,1)}, u32[]{:S(2)}) copy-start(bf16[128,64,2,2,2]{0,4,3,2,1:T(2,128)(2,1)} %param.10) | copy-start | bytes 393220
  2.9 5.3 %collective-permute-start.1 = (bf16[2,2,64,128]{3,2,1,0:T(8,128)(2,1)S(1)}, bf16[2,2,64,128]{3,2,1,0:T(8,128)(2,1)S(1)}, u32[]{:S(2)}, u32[]{:S(2)}) collective-permute-start(bf16[2,2,64,128]{3,2,1,0:T(8,128)(2,1)S(1)} %get-tuple-element.32), channel_id=1, source_target_pairs={{0,1},{1,0},{2,3},{3,2},{4,5},{5,4},{6,7},{7,6},{8,9},{9,8},{10,11... | collective-permute-start | bytes 196616 | tf_op jit(solution)/shard_map/ppermute | solution.py:60
  6.0 5.7 %collective-permute-start.4 = (bf16[1,1,256,128]{3,2,1,0:T(8,128)(2,1)S(1)}, bf16[1,1,256,128]{3,2,1,0:T(8,128)(2,1)S(1)}, u32[]{:S(2)}, u32[]{:S(2)}) collective-permute-start(bf16[1,1,256,128]{3,2,1,0:T(8,128)(2,1)S(1)} %dynamic-slice_bitcast_fusion), channel_id=1, source_target_pairs={{0,4},{4,0},{8,12},{12,8},{16,20},{20,16},{24,28},{28,24},{1,5},{5... | collective-permute-start | bytes 196616 | tf_op jit(solution)/shard_map/ppermute | solution.py:516
  6.1 2.2 %collective-permute-start.2 = (bf16[2,2,64,128]{3,2,1,0:T(8,128)(2,1)S(1)}, bf16[2,2,64,128]{3,2,1,0:T(8,128)(2,1)S(1)}, u32[]{:S(2)}, u32[]{:S(2)}) collective-permute-start(bf16[2,2,64,128]{3,2,1,0:T(8,128)(2,1)S(1)} %get-tuple-element.33), channel_id=1, source_target_pairs={{1,2},{2,1},{5,6},{6,5},{9,10},{10,9},{13,14},{14,13},{17,18},{18,... | collective-permute-start | bytes 196616 | tf_op jit(solution)/shard_map/ppermute | solution.py:60
  6.8 6.3 %collective-permute-start.5 = (bf16[2,8,64,128]{3,2,1,0:T(8,128)(2,1)S(1)}, bf16[2,8,64,128]{3,2,1,0:T(8,128)(2,1)S(1)}, u32[]{:S(2)}, u32[]{:S(2)}) collective-permute-start(bf16[2,8,64,128]{3,2,1,0:T(8,128)(2,1)S(1)} %get-tuple-element.30.refs_1_.refs_0_), channel_id=1, source_target_pairs={{0,4},{4,0},{8,12},{12,8},{16,20},{20,16},{24,28},{28,24},{1,5},{5... | collective-permute-start | bytes 786440 | tf_op jit(solution)/shard_map/ppermute | solution.py:56
  7.3 9.9 %collective-permute-start = (bf16[2,8,64,128]{3,2,1,0:T(8,128)(2,1)S(1)}, bf16[2,8,64,128]{3,2,1,0:T(8,128)(2,1)S(1)}, u32[]{:S(2)}, u32[]{:S(2)}) collective-permute-start(bf16[2,8,64,128]{3,2,1,0:T(8,128)(2,1)S(1)} %get-tuple-element.31.refs_2_.refs_1_), channel_id=1, source_target_pairs={{4,8},{8,4},{12,16},{16,12},{20,24},{24,20},{5,9},{9,5},{13,17},{1... | collective-permute-start | bytes 786440 | tf_op jit(solution)/shard_map/ppermute | solution.py:56
  8.3 4.7 %collective-permute-start.6 = (bf16[2,2,64,128]{3,2,1,0:T(8,128)(2,1)S(1)}, bf16[2,2,64,128]{3,2,1,0:T(8,128)(2,1)S(1)}, u32[]{:S(2)}, u32[]{:S(2)}) collective-permute-start(bf16[2,2,64,128]{3,2,1,0:T(8,128)(2,1)S(1)} %pad_maximum_fusion.3), channel_id=1, source_target_pairs={{0,4},{4,0},{8,12},{12,8},{16,20},{20,16},{24,28},{28,24},{1,5},{5... | collective-permute-start | bytes 196616 | tf_op jit(solution)/shard_map/ppermute | solution.py:56
  11.0 6.1 %collective-permute-start.3 = (bf16[2,2,64,128]{3,2,1,0:T(8,128)(2,1)S(1)}, bf16[2,2,64,128]{3,2,1,0:T(8,128)(2,1)S(1)}, u32[]{:S(2)}, u32[]{:S(2)}) collective-permute-start(bf16[2,2,64,128]{3,2,1,0:T(8,128)(2,1)S(1)} %pad_maximum_fusion.2), channel_id=1, source_target_pairs={{4,8},{8,4},{12,16},{16,12},{20,24},{24,20},{5,9},{9,5},{13,17},{1... | collective-permute-start | bytes 196616 | tf_op jit(solution)/shard_map/ppermute | solution.py:56
  11.8 1.3 %copy-start.2 = (bf16[256,64]{0,1:T(8,128)(2,1)S(1)}, bf16[256,64]{0,1:T(8,128)(2,1)}, u32[]{:S(2)}) copy-start(bf16[256,64]{0,1:T(8,128)(2,1)} %param.8) | copy-start | bytes 98308
  11.8 1.3 %copy-start.3 = (bf16[64,256]{1,0:T(8,128)(2,1)S(1)}, bf16[64,256]{1,0:T(8,128)(2,1)}, u32[]{:S(2)}) copy-start(bf16[64,256]{1,0:T(8,128)(2,1)} %refs_9_.3) | copy-start | bytes 98308
  22.5 18.7 %collective-permute-start.8 = (bf16[2,8,64,128]{3,2,1,0:T(8,128)(2,1)S(1)}, bf16[2,8,64,128]{3,2,1,0:T(8,128)(2,1)S(1)}, u32[]{:S(2)}, u32[]{:S(2)}) collective-permute-start(bf16[2,8,64,128]{3,2,1,0:T(8,128)(2,1)S(1)} %get-tuple-element.45.refs_0_), channel_id=1, source_target_pairs={{0,4},{4,0},{8,12},{12,8},{16,20},{20,16},{24,28},{28,24},{1,5},{5... | collective-permute-start | bytes 786440 | tf_op jit(solution)/shard_map/ppermute | solution.py:56
  25.4 9.7 %all-to-all-start = ((bf16[8,104,128]{2,1,0:T(8,128)(2,1)}), bf16[8,104,128]{2,1,0:T(8,128)(2,1)S(1)}, u32[]{:S(2)}, u32[]{:S(2)}) async-start(bf16[8,104,128]{2,1,0:T(8,128)(2,1)} %bitcast.22), calls=%async_computation | async-start | bytes 425984 | tf_op jit(solution)/shard_map/all_to_all | solution.py:644
  28.8 12.5 %collective-permute-start.9 = (bf16[2,8,64,128]{3,2,1,0:T(8,128)(2,1)S(1)}, bf16[2,8,64,128]{3,2,1,0:T(8,128)(2,1)S(1)}, u32[]{:S(2)}, u32[]{:S(2)}) collective-permute-start(bf16[2,8,64,128]{3,2,1,0:T(8,128)(2,1)S(1)} %get-tuple-element.46.refs_1_), channel_id=1, source_target_pairs={{4,8},{8,4},{12,16},{16,12},{20,24},{24,20},{5,9},{9,5},{13,17},{1... | collective-permute-start | bytes 786440 | tf_op jit(solution)/shard_map/ppermute | solution.py:56
  29.5 21.7 %collective-permute-start.7 = (bf16[1,1,256,128]{3,2,1,0:T(8,128)(2,1)S(1)}, bf16[1,1,256,128]{3,2,1,0:T(8,128)(2,1)S(1)}, u32[]{:S(2)}, u32[]{:S(2)}) collective-permute-start(bf16[1,1,256,128]{3,2,1,0:T(8,128)(2,1)S(1)} %constant_dynamic-slice_fusion), channel_id=1, source_target_pairs={{0,4},{4,0},{8,12},{12,8},{16,20},{20,16},{24,28},{28,24},{1,5},{5... | collective-permute-start | bytes 196616 | tf_op jit(solution)/shard_map/ppermute | solution.py:516
  35.8 11.3 %all-to-all-start.1 = ((bf16[4,104,128]{2,1,0:T(8,128)(2,1)}), bf16[4,104,128]{2,1,0:T(8,128)(2,1)S(1)}, u32[]{:S(2)}, u32[]{:S(2)}) async-start(bf16[4,104,128]{2,1,0:T(8,128)(2,1)} %sum_spread.2), calls=%async_computation.1 | async-start | bytes 212992 | tf_op jit(solution)/shard_map/all_to_all | solution.py:645
  41.3 10.6 %collective-permute-start.11 = (bf16[4,2,64,128]{3,2,1,0:T(8,128)(2,1)S(1)}, bf16[4,2,64,128]{3,2,1,0:T(8,128)(2,1)S(1)}, u32[]{:S(2)}, u32[]{:S(2)}) collective-permute-start(bf16[4,2,64,128]{3,2,1,0:T(8,128)(2,1)S(1)} %pad_maximum_fusion.1), channel_id=1, source_target_pairs={{1,2},{2,1},{5,6},{6,5},{9,10},{10,9},{13,14},{14,13},{17,18},{18,... | collective-permute-start | bytes 393224 | tf_op jit(solution)/shard_map/ppermute | solution.py:60
  42.0 9.9 %collective-permute-start.10 = (bf16[4,2,64,128]{3,2,1,0:T(8,128)(2,1)S(1)}, bf16[4,2,64,128]{3,2,1,0:T(8,128)(2,1)S(1)}, u32[]{:S(2)}, u32[]{:S(2)}) collective-permute-start(bf16[4,2,64,128]{3,2,1,0:T(8,128)(2,1)S(1)} %pad_maximum_fusion), channel_id=1, source_target_pairs={{0,1},{1,0},{2,3},{3,2},{4,5},{5,4},{6,7},{7,6},{8,9},{9,8},{10,11... | collective-permute-start | bytes 393224 | tf_op jit(solution)/shard_map/ppermute | solution.py:60
  47.8 9.7 %all-to-all-start.2 = ((bf16[8,104,128]{2,1,0:T(8,128)(2,1)}), bf16[8,104,128]{2,1,0:T(8,128)(2,1)S(1)}, u32[]{:S(2)}, u32[]{:S(2)}) async-start(bf16[8,104,128]{2,1,0:T(8,128)(2,1)} %sum_spread.3), calls=%async_computation.2 | async-start | bytes 425984 | tf_op jit(solution)/shard_map/all_to_all | solution.py:648
